TPU v7x, 256 devices: a whole 4x4x8 slice. The times are simulated.
256 devices in a mesh: ctx: 16 (over y, x), tp: 16 (over z, core).
Axes of the slice: x: 4, y: 4, z: 8, core: 2. Of those that a mesh axis runs over, the one named last changes fastest.
Arguments:
- queries: bfloat16 [8192, 16384], P(('ctx', 'tp')), may hold values from -4.5 to 4.5
- key_vectors: bfloat16 [8192, 1024], P(('ctx', 'tp')), may hold values from -5 to 5
- value_vectors: bfloat16 [8192, 1024], P(('ctx', 'tp')), may hold values from -6 to 6
- output_cotangent: bfloat16 [8192, 16384], P(('ctx', 'tp')), may hold values from -6 to 6
- doc_lengths: int32 [16], replicated, may hold values from 1 to 1025, as said below
Outputs:
- attended: bfloat16 [8192, 16384], P(('ctx', 'tp'))
- query_gradient: bfloat16 [8192, 16384], P(('ctx', 'tp'))
- key_gradient: bfloat16 [8192, 1024], P(('ctx', 'tp'))
- value_gradient: bfloat16 [8192, 1024], P(('ctx', 'tp'))
Inputs may be any that keep to these rules, and one draw needn't show every extreme that they name: `doc_lengths`: the 16 lengths sum to 8192; exactly one of them equals 1025.
All inputs are finite; a program needn't handle non-finite values.
Results may differ from a plain program's by a relative error of at most 0.02.
Values may be sent and summed in bfloat16 or wider, within the bound.
No kernel may reach another device: no remote copies, remote signals or barrier semaphores. Data moves between devices by JAX's collectives and lax.ppermute only.
A program may use at most 192 MiB of HBM per device.

v0:
```python
import functools
import math

import jax
import jax.numpy as jnp
from jax import lax
from jax.experimental import pallas as pl
from jax.experimental.pallas import tpu as pltpu
from jax.sharding import Mesh, PartitionSpec as P

HEAD_DIM = 128
KV_HEADS = 8
GROUP = 16
NDOC = 16
CHUNK = 64
RING = 8
ROW = 4
UNITS = ROW + 2
REACH = 16
WINDOW = (REACH + 1) * CHUNK
CLASSES = (17, 13, 11, 9, 7, 5, 3)
HEADS_STEP = 16
ROWS_STEP = HEADS_STEP * CHUNK
MASK_FILL = -1e30
SCALE = 1.0 / math.sqrt(HEAD_DIM)
SCALE_LOG2 = SCALE * math.log2(math.e)
BF16 = jnp.bfloat16
F32 = jnp.float32
HEAD_AXES = ("x", "core")
WIDE = GROUP * HEAD_DIM


def dot_t(a, b):
    return lax.dot_general(a, b, (((1,), (1,)), ((), ())), preferred_element_type=F32)


def dot(a, b):
    return jnp.dot(a, b, preferred_element_type=F32)


def attention_kernel(place, lengths, qdo_ref, *refs):
    kv_refs = refs[:RING]
    v4_ref = refs[RING]
    odq_ref = refs[RING + 1]
    dkv_refs = refs[RING + 2 : 2 * RING + 2]
    dv4_ref = refs[2 * RING + 2]
    kwin, vwin, dwin, acc = refs[2 * RING + 3 :]
    step = pl.program_id(0)
    z = place[1]
    first = ((place[0] * ROW + step) * RING + z) * CHUNK
    base = first - REACH * CHUNK

    @pl.when(step == 0)
    def _():
        acc[...] = jnp.zeros_like(acc)

    def unit(t):
        return step + t // RING + (z + t % RING >= RING).astype(jnp.int32)

    tokens = first + lax.broadcasted_iota(jnp.int32, (CHUNK, 1), 0)
    starts = jnp.zeros((CHUNK, 1), jnp.int32)
    ending = jnp.int32(0)
    earliest = jnp.int32(0)
    for d in range(NDOC):
        ending = ending + lengths[d]
        starts = jnp.where(tokens >= ending, ending, starts)
        earliest = jnp.where(first >= ending, ending, earliest)
    needed = REACH + 1 - (earliest - base) // CHUNK

    def run(chunks):
        skipped = REACH + 1 - chunks
        width = chunks * CHUNK
        for t in range(skipped, REACH + 1):
            at = (t - skipped) * CHUNK
            slot = t % RING
            if slot == RING // 2:
                kwin[at : at + CHUNK, :] = kv_refs[slot][unit(t)]
                vwin[at : at + CHUNK, :] = v4_ref[unit(t)]
            else:
                pair = kv_refs[slot][unit(t)]
                kwin[at : at + CHUNK, :] = pair[:, :HEAD_DIM]
                vwin[at : at + CHUNK, :] = pair[:, HEAD_DIM:]
        columns = base + skipped * CHUNK + lax.broadcasted_iota(jnp.int32, (CHUNK, width), 1)
        allowed = (columns >= starts) & (columns <= tokens)
        bias = jnp.where(allowed, 0.0, MASK_FILL).astype(F32)[None]
        dwin[:, :width] = jnp.zeros((2 * HEAD_DIM, width), F32)

        def block(number, carry):
            lanes = pl.multiple_of(number * (HEADS_STEP * HEAD_DIM), HEADS_STEP * HEAD_DIM)
            span = pl.ds(lanes, HEADS_STEP * HEAD_DIM)
            other = pl.ds(WIDE + lanes, HEADS_STEP * HEAD_DIM)
            q_all = qdo_ref[:, span]
            do_all = qdo_ref[:, other]

            def stack(block_all):
                return jnp.concatenate(
                    [block_all[:, h * HEAD_DIM : (h + 1) * HEAD_DIM] for h in range(HEADS_STEP)], 0
                )

            def unstack(rows):
                return jnp.concatenate(
                    [rows[h * CHUNK : (h + 1) * CHUNK] for h in range(HEADS_STEP)], 1
                )

            q = stack(q_all)
            do = stack(do_all)
            keys = kwin[:width, :]
            values = vwin[:width, :]
            scores = (dot_t(q, keys) * SCALE_LOG2).reshape(HEADS_STEP, CHUNK, width) + bias
            scores = scores.reshape(ROWS_STEP, width)
            highest = jnp.max(scores, axis=-1, keepdims=True)
            powers = jnp.exp2(scores - highest)
            total = jnp.sum(powers, axis=-1, keepdims=True)
            probabilities = powers * (1.0 / total)
            weights = probabilities.astype(BF16)
            attended = dot(weights, values).astype(BF16)
            delta = jnp.sum(do.astype(F32) * attended.astype(F32), axis=-1, keepdims=True)
            slopes = (probabilities * (dot_t(do, values) - delta)).astype(BF16)
            odq_ref[:, span] = unstack(attended)
            odq_ref[:, other] = unstack((dot(slopes, keys) * SCALE).astype(BF16))
            dwin[:HEAD_DIM, :width] += dot(q.astype(F32).T.astype(BF16), slopes)
            dwin[HEAD_DIM:, :width] += dot(do.astype(F32).T.astype(BF16), weights)
            return carry

        lax.fori_loop(0, GROUP // HEADS_STEP, block, 0)
        back = dwin[:, :width].T
        for t in range(skipped, REACH + 1):
            at = (t - skipped) * CHUNK
            acc[t % RING, unit(t)] += back[at : at + CHUNK, :]

    for index, chunks in enumerate(CLASSES):
        fits = needed <= chunks
        if index == 0:
            fits = needed > CLASSES[1]
        elif index + 1 < len(CLASSES):
            fits = fits & (needed > CLASSES[index + 1])
        pl.when(fits)(functools.partial(run, chunks))

    @pl.when(step == ROW - 1)
    def _():
        for slot in range(RING):
            whole = acc[slot]
            keys_part = (whole[:, :, :HEAD_DIM] * SCALE).astype(BF16)
            values_part = whole[:, :, HEAD_DIM:].astype(BF16)
            if slot == RING // 2:
                dkv_refs[slot][...] = keys_part
                dv4_ref[...] = values_part
            else:
                dkv_refs[slot][:, :, :HEAD_DIM] = keys_part
                dkv_refs[slot][:, :, HEAD_DIM:] = values_part


def attention(place, lengths, qdo, slots, v4):
    rows = pl.BlockSpec((CHUNK, 2 * WIDE), lambda i, *_: (i, 0))

    def whole(shape):
        return pl.BlockSpec(shape, lambda i, *_: (0, 0, 0))

    pair = (UNITS, CHUNK, 2 * HEAD_DIM)
    single = (UNITS, CHUNK, HEAD_DIM)
    shapes = [single if slot == RING // 2 else pair for slot in range(RING)] + [single]
    kv_specs = [whole(shape) for shape in shapes]
    big = jax.ShapeDtypeStruct((ROW * CHUNK, 2 * WIDE), BF16)
    return pl.pallas_call(
        attention_kernel,
        out_shape=[big] + [jax.ShapeDtypeStruct(shape, BF16) for shape in shapes],
        grid_spec=pltpu.PrefetchScalarGridSpec(
            num_scalar_prefetch=2,
            grid=(ROW,),
            in_specs=[rows] + kv_specs,
            out_specs=[rows] + kv_specs,
            scratch_shapes=[
                pltpu.VMEM((WINDOW, HEAD_DIM), BF16),
                pltpu.VMEM((WINDOW, HEAD_DIM), BF16),
                pltpu.VMEM((2 * HEAD_DIM, WINDOW), F32),
                pltpu.VMEM((RING, UNITS, CHUNK, 2 * HEAD_DIM), F32),
            ],
        ),
        compiler_params=pltpu.CompilerParams(vmem_limit_bytes=56 * 1024 * 1024),
    )(place, lengths, qdo, *slots, v4)


def around(value, step):
    return lax.ppermute(value, "z", [(i, (i + step) % RING) for i in range(RING)])


def exchanged(value):
    return lax.all_to_all(value, HEAD_AXES, split_axis=0, concat_axis=0, tiled=True)


def split_kernel(a_ref, b_ref, out_ref):
    width = out_ref.shape[2] // 2
    for g in range(out_ref.shape[0]):
        out_ref[g, :, :width] = a_ref[:, g * width : (g + 1) * width]
        out_ref[g, :, width:] = b_ref[:, g * width : (g + 1) * width]


def split_heads(a, b, steps):
    rows, width = a.shape[0], a.shape[1] // KV_HEADS
    count = KV_HEADS // steps
    part = pl.BlockSpec((rows, count * width), lambda g: (0, g))
    return pl.pallas_call(
        split_kernel,
        out_shape=jax.ShapeDtypeStruct((KV_HEADS, rows, 2 * width), a.dtype),
        grid=(steps,),
        in_specs=[part, part],
        out_specs=pl.BlockSpec((count, rows, 2 * width), lambda g: (g, 0, 0)),
    )(a, b)


def merge_kernel(in_ref, a_ref, b_ref):
    width = in_ref.shape[2] // 2
    for g in range(in_ref.shape[0]):
        a_ref[:, g * width : (g + 1) * width] = in_ref[g, :, :width]
        b_ref[:, g * width : (g + 1) * width] = in_ref[g, :, width:]


def merge_heads(value, steps):
    groups, rows, width = value.shape[0], value.shape[1], value.shape[2] // 2
    count = groups // steps
    part = pl.BlockSpec((rows, count * width), lambda g: (0, g))
    whole = jax.ShapeDtypeStruct((rows, groups * width), value.dtype)
    return pl.pallas_call(
        merge_kernel,
        out_shape=[whole, whole],
        grid=(steps,),
        in_specs=[pl.BlockSpec((count, rows, 2 * width), lambda g: (g, 0, 0))],
        out_specs=[part, part],
    )(value)


def added(a, b):
    return (a.astype(F32) + b.astype(F32)).astype(BF16)


def body(queries, key_vectors, value_vectors, output_cotangent, doc_lengths):
    local = key_vectors.shape[0]
    tokens = KV_HEADS * local
    own = exchanged(split_heads(key_vectors, value_vectors, 1)).reshape(tokens, 2 * HEAD_DIM)
    qdo = exchanged(split_heads(queries, output_cotangent, 2)).reshape(tokens, 2 * WIDE)
    half = 2 * CHUNK
    earlier = lax.ppermute(own[half:], "y", [(i, i + 1) for i in range(ROW - 1)])
    units = jnp.concatenate([earlier, own], axis=0)
    middle = RING // 2
    slots = [None] * RING
    slots[0] = units
    up = down = units
    for step in range(1, middle):
        up, down = around(up, 1), around(down, -1)
        slots[RING - step], slots[step] = up, down
    up, down, qdo = lax.optimization_barrier((up, down, qdo))
    slots[middle] = around(up[:, :HEAD_DIM], 1)
    last_values = around(down[:, HEAD_DIM:], -1)
    place = jnp.stack([lax.axis_index("y"), lax.axis_index("z")]).astype(jnp.int32)
    slots = [s.reshape(UNITS, CHUNK, -1) for s in slots]
    results = attention(
        place, doc_lengths, qdo, slots, last_values.reshape(UNITS, CHUNK, HEAD_DIM)
    )
    odq = exchanged(results[0].reshape(KV_HEADS, local, 2 * WIDE))
    parts = [r.reshape(UNITS * CHUNK, -1) for r in results[1:]]
    up = around(parts[middle], 1)
    down = around(parts[RING], -1)
    up = jnp.concatenate(
        [added(parts[middle - 1][:, :HEAD_DIM], up), parts[middle - 1][:, HEAD_DIM:]], 1
    )
    down = jnp.concatenate(
        [parts[middle + 1][:, :HEAD_DIM], added(parts[middle + 1][:, HEAD_DIM:], down)], 1
    )
    for step in range(middle - 2, 0, -1):
        up = added(parts[step], around(up, 1))
        down = added(parts[RING - step], around(down, -1))
    mine = parts[0].astype(F32) + around(up, 1).astype(F32) + around(down, -1).astype(F32)
    returned = lax.ppermute(mine[:half].astype(BF16), "y", [(i, i - 1) for i in range(1, ROW)])
    total = jnp.concatenate([mine[half : 2 * half], mine[2 * half :] + returned.astype(F32)], 0)
    total = total.astype(BF16).reshape(KV_HEADS, local, 2 * HEAD_DIM)
    total, odq = lax.optimization_barrier((total, odq))
    attended, query_slope = merge_heads(odq, 2)
    key_slope, value_slope = merge_heads(exchanged(total), 1)
    return attended, query_slope, key_slope, value_slope


def solution(mesh):
    split = Mesh(mesh.devices.reshape(ROW, ROW, RING, 2), ("y", "x", "z", "core"))
    rows = P(("y", "x", "z", "core"), None)
    return jax.shard_map(
        body,
        mesh=split,
        in_specs=(rows, rows, rows, rows, P()),
        out_specs=(rows, rows, rows, rows),
        check_vma=False,
    )
```

profile of v0, /device:TPU:16, one launch (start us, length us, event | category | flops | bytes accessed | tf_op | source)
XLA Modules:
  0.0 124.1 jit_solution(4038508716573015555)
XLA Ops:
  2.2 4.3 %all-to-all-start = ((bf16[8,32,256]{2,1,0:T(8,128)(2,1)}), bf16[8,32,256]{2,1,0:T(8,128)(2,1)S(1)}, u32[]{:S(2)}, u32[]{:S(2)}) async-start(bf16[8,32,256]{2,1,0:T(8,128)(2,1)} %shard_map.84), calls=%async_computation | async-start | bytes 262144 | tf_op jit(solution)/shard_map/all_to_all | solution.py:188
  6.5 2.6 %shard_map.85 = bf16[8,32,4096]{2,1,0:T(8,128)(2,1)} custom-call(bf16[32,16384]{1,0:T(8,128)(2,1)} %a_ref.3, bf16[32,16384]{1,0:T(8,128)(2,1)} %b_ref.3), custom_call_target="tpu_custom_call" | custom-call | tf_op jit(solution)/shard_map/pallas_call | solution.py:202
  9.1 3.5 %all-to-all-done = bf16[8,32,256]{2,1,0:T(8,128)(2,1)S(1)} async-done(((bf16[8,32,256]{2,1,0:T(8,128)(2,1)}), bf16[8,32,256]{2,1,0:T(8,128)(2,1)S(1)}, u32[]{:S(2)}, u32[]{:S(2)}) %all-to-all-start) | async-done | bytes 131104 | tf_op jit(solution)/shard_map/all_to_all | solution.py:188
  12.6 3.6 %all-to-all-start.1 = ((bf16[8,32,4096]{2,1,0:T(8,128)(2,1)}), bf16[8,32,4096]{2,1,0:T(8,128)(2,1)S(1)}, u32[]{:S(2)}, u32[]{:S(2)}) async-start(bf16[8,32,4096]{2,1,0:T(8,128)(2,1)} %shard_map.85), calls=%async_computation.1 | async-start | bytes 4194304 | tf_op jit(solution)/shard_map/all_to_all | solution.py:188
  16.2 3.2 %collective-permute-start = (bf16[128,256]{1,0:T(8,128)(2,1)S(1)}, bf16[128,256]{1,0:T(8,128)(2,1)S(1)}, u32[]{:S(2)}, u32[]{:S(2)}) collective-permute-start(bf16[128,256]{1,0:T(8,128)(2,1)S(1)} %bitcast.52), channel_id=1, source_target_pairs={{0,64},{64,128},{128,192},{1,65},{65,129},{129,193},{2,66},{66,130... | collective-permute-start | bytes 196616 | tf_op jit(solution)/shard_map/ppermute | solution.py:242
  19.4 3.1 %collective-permute-done = bf16[128,256]{1,0:T(8,128)(2,1)S(1)} collective-permute-done((bf16[128,256]{1,0:T(8,128)(2,1)S(1)}, bf16[128,256]{1,0:T(8,128)(2,1)S(1)}, u32[]{:S(2)}, u32[]{:S(2)}) %collective-permute-start) | collective-permute-done | bytes 65568 | tf_op jit(solution)/shard_map/ppermute | solution.py:242
  22.6 5.9 %collective-permute-start.4 = (bf16[384,256]{1,0:T(8,128)(2,1)S(1)}, bf16[384,256]{1,0:T(8,128)(2,1)S(1)}, u32[]{:S(2)}, u32[]{:S(2)}) collective-permute-start(bf16[384,256]{1,0:T(8,128)(2,1)S(1)} %pad_maximum_fusion), channel_id=1, source_target_pairs={{0,14},{2,0},{4,2},{6,4},{8,6},{10,8},{12,10},{14,12},{1,15},{3,1}... | collective-permute-start | bytes 589832 | tf_op jit(solution)/shard_map/ppermute | solution.py:184
  28.5 4.0 %collective-permute-done.4 = bf16[384,256]{1,0:T(8,128)(2,1)S(1)} collective-permute-done((bf16[384,256]{1,0:T(8,128)(2,1)S(1)}, bf16[384,256]{1,0:T(8,128)(2,1)S(1)}, u32[]{:S(2)}, u32[]{:S(2)}) %collective-permute-start.4) | collective-permute-done | bytes 196640 | tf_op jit(solution)/shard_map/ppermute | solution.py:184
  32.5 3.7 %collective-permute-start.5 = (bf16[384,256]{1,0:T(8,128)(2,1)S(1)}, bf16[384,256]{1,0:T(8,128)(2,1)S(1)}, u32[]{:S(2)}, u32[]{:S(2)}) collective-permute-start(bf16[384,256]{1,0:T(8,128)(2,1)S(1)} %collective-permute-done.4), channel_id=1, source_target_pairs={{0,14},{2,0},{4,2},{6,4},{8,6},{10,8},{12,10},{14,12},{1,15},{3,1}... | collective-permute-start | bytes 589832 | tf_op jit(solution)/shard_map/ppermute | solution.py:184
  36.2 3.2 %collective-permute-done.5 = bf16[384,256]{1,0:T(8,128)(2,1)S(1)} collective-permute-done((bf16[384,256]{1,0:T(8,128)(2,1)S(1)}, bf16[384,256]{1,0:T(8,128)(2,1)S(1)}, u32[]{:S(2)}, u32[]{:S(2)}) %collective-permute-start.5) | collective-permute-done | bytes 196640 | tf_op jit(solution)/shard_map/ppermute | solution.py:184
  39.4 3.7 %collective-permute-start.6 = (bf16[384,256]{1,0:T(8,128)(2,1)S(1)}, bf16[384,256]{1,0:T(8,128)(2,1)S(1)}, u32[]{:S(2)}, u32[]{:S(2)}) collective-permute-start(bf16[384,256]{1,0:T(8,128)(2,1)S(1)} %collective-permute-done.5), channel_id=1, source_target_pairs={{0,14},{2,0},{4,2},{6,4},{8,6},{10,8},{12,10},{14,12},{1,15},{3,1}... | collective-permute-start | bytes 589832 | tf_op jit(solution)/shard_map/ppermute | solution.py:184
  43.1 3.2 %collective-permute-done.6 = bf16[384,256]{1,0:T(8,128)(2,1)S(1)} collective-permute-done((bf16[384,256]{1,0:T(8,128)(2,1)S(1)}, bf16[384,256]{1,0:T(8,128)(2,1)S(1)}, u32[]{:S(2)}, u32[]{:S(2)}) %collective-permute-start.6) | collective-permute-done | bytes 196640 | tf_op jit(solution)/shard_map/ppermute | solution.py:184
  46.3 3.7 %collective-permute-done.3 = bf16[384,256]{1,0:T(8,128)(2,1)S(1)} collective-permute-done((bf16[384,256]{1,0:T(8,128)(2,1)S(1)}, bf16[384,256]{1,0:T(8,128)(2,1)S(1)}, u32[]{:S(2)}, u32[]{:S(2)}) %collective-permute-start.3) | collective-permute-done | bytes 196640 | tf_op jit(solution)/shard_map/ppermute | solution.py:184
  56.6 12.3 %shard_map.86 = (bf16[256,4096]{1,0:T(8,128)(2,1)}, bf16[6,64,256]{2,1,0:T(8,128)(2,1)}, bf16[6,64,256]{2,1,0:T(8,128)(2,1)}, bf16[6,64,256]{2,1,0:T(8,128)(2,1)...) custom-call(s32[2]{0:T(128)} %pad_add_fusion.place, ...), custom_call_target="tpu_custom_call" | custom-call | tf_op jit(solution)/shard_map/pallas_call | solution.py:164
  69.4 4.4 %all-to-all-start.2 = ((bf16[8,32,4096]{2,1,0:T(8,128)(2,1)}), bf16[8,32,4096]{2,1,0:T(8,128)(2,1)S(1)}, u32[]{:S(2)}, u32[]{:S(2)}) async-start(bf16[8,32,4096]{2,1,0:T(8,128)(2,1)} %bitcast.37), calls=%async_computation.2 | async-start | bytes 4194304 | tf_op jit(solution)/shard_map/all_to_all | solution.py:188
  77.3 3.0 %collective-permute-done.9 = bf16[384,128]{1,0:T(8,128)(2,1)S(1)} collective-permute-done((bf16[384,128]{1,0:T(8,128)(2,1)S(1)}, bf16[384,128]{1,0:T(8,128)(2,1)S(1)}, u32[]{:S(2)}, u32[]{:S(2)}) %collective-permute-start.9) | collective-permute-done | bytes 98336 | tf_op jit(solution)/shard_map/ppermute | solution.py:184
  82.8 2.9 %collective-permute-start.15 = (bf16[384,256]{1,0:T(8,128)(2,1)S(1)}, bf16[384,256]{1,0:T(8,128)(2,1)S(1)}, u32[]{:S(2)}, u32[]{:S(2)}) collective-permute-start(bf16[384,256]{1,0:T(8,128)(2,1)S(1)} %fusion), channel_id=1, source_target_pairs={{0,14},{2,0},{4,2},{6,4},{8,6},{10,8},{12,10},{14,12},{1,15},{3,1}... | collective-permute-start | bytes 589832 | tf_op jit(solution)/shard_map/ppermute | solution.py:184
  85.7 2.5 %collective-permute-done.10 = bf16[384,256]{1,0:T(8,128)(2,1)S(1)} collective-permute-done((bf16[384,256]{1,0:T(8,128)(2,1)S(1)}, bf16[384,256]{1,0:T(8,128)(2,1)S(1)}, u32[]{:S(2)}, u32[]{:S(2)}) %collective-permute-start.10) | collective-permute-done | bytes 196640 | tf_op jit(solution)/shard_map/ppermute | solution.py:184
  89.5 3.8 %collective-permute-start.16 = (bf16[384,256]{1,0:T(8,128)(2,1)S(1)}, bf16[384,256]{1,0:T(8,128)(2,1)S(1)}, u32[]{:S(2)}, u32[]{:S(2)}) collective-permute-start(bf16[384,256]{1,0:T(8,128)(2,1)S(1)} %fusion.1), channel_id=1, source_target_pairs={{0,14},{2,0},{4,2},{6,4},{8,6},{10,8},{12,10},{14,12},{1,15},{3,1}... | collective-permute-start | bytes 589832 | tf_op jit(solution)/shard_map/ppermute | solution.py:184
  96.4 5.8 %collective-permute-done.12 = bf16[384,256]{1,0:T(8,128)(2,1)S(1)} collective-permute-done((bf16[384,256]{1,0:T(8,128)(2,1)S(1)}, bf16[384,256]{1,0:T(8,128)(2,1)S(1)}, u32[]{:S(2)}, u32[]{:S(2)}) %collective-permute-start.12) | collective-permute-done | bytes 196640 | tf_op jit(solution)/shard_map/ppermute | solution.py:184
  102.4 6.8 %collective-permute-start.17 = (bf16[128,256]{1,0:T(8,128)(2,1)S(1)}, bf16[128,256]{1,0:T(8,128)(2,1)S(1)}, u32[]{:S(2)}, u32[]{:S(2)}) collective-permute-start(bf16[128,256]{1,0:T(8,128)(2,1)S(1)} %get-tuple-element.45), channel_id=1, source_target_pairs={{64,0},{128,64},{192,128},{65,1},{129,65},{193,129},{66,2},{130,66... | collective-permute-start | bytes 196616 | tf_op jit(solution)/shard_map/ppermute | solution.py:273
  111.7 4.1 %all-to-all-start.3 = ((bf16[8,32,256]{2,1,0:T(8,128)(2,1)}), bf16[8,32,256]{2,1,0:T(8,128)(2,1)S(1)}, u32[]{:S(2)}, u32[]{:S(2)}) async-start(bf16[8,32,256]{2,1,0:T(8,128)(2,1)} %bitcast.23), calls=%async_computation.3 | async-start | bytes 262144 | tf_op jit(solution)/shard_map/all_to_all | solution.py:188
  115.8 2.6 %shard_map.87 = (bf16[32,16384]{1,0:T(8,128)(2,1)}, bf16[32,16384]{1,0:T(8,128)(2,1)}) custom-call(bf16[8,32,4096]{2,1,0:T(8,128)(2,1)} %copy-done), custom_call_target="tpu_custom_call" | custom-call | tf_op jit(solution)/shard_map/pallas_call | solution.py:223
  118.4 3.5 %all-to-all-done.3.in_ref = bf16[8,32,256]{2,1,0:T(8,128)(2,1)S(1)} async-done(((bf16[8,32,256]{2,1,0:T(8,128)(2,1)}), bf16[8,32,256]{2,1,0:T(8,128)(2,1)S(1)}, u32[]{:S(2)}, u32[]{:S(2)}) %all-to-all-start.3) | async-done | bytes 131104 | tf_op jit(solution)/shard_map/all_to_all | solution.py:188
  (84 shorter events, 23.9 us)
Async XLA Ops:
  2.2 10.4 %all-to-all-start = ((bf16[8,32,256]{2,1,0:T(8,128)(2,1)}), bf16[8,32,256]{2,1,0:T(8,128)(2,1)S(1)}, u32[]{:S(2)}, u32[]{:S(2)}) async-start(bf16[8,32,256]{2,1,0:T(8,128)(2,1)} %shard_map.84), calls=%async_computation | async-start | bytes 262144 | tf_op jit(solution)/shard_map/all_to_all | solution.py:188
  12.6 37.3 %all-to-all-start.1 = ((bf16[8,32,4096]{2,1,0:T(8,128)(2,1)}), bf16[8,32,4096]{2,1,0:T(8,128)(2,1)S(1)}, u32[]{:S(2)}, u32[]{:S(2)}) async-start(bf16[8,32,4096]{2,1,0:T(8,128)(2,1)} %shard_map.85), calls=%async_computation.1 | async-start | bytes 4194304 | tf_op jit(solution)/shard_map/all_to_all | solution.py:188
  16.2 6.3 %collective-permute-start = (bf16[128,256]{1,0:T(8,128)(2,1)S(1)}, bf16[128,256]{1,0:T(8,128)(2,1)S(1)}, u32[]{:S(2)}, u32[]{:S(2)}) collective-permute-start(bf16[128,256]{1,0:T(8,128)(2,1)S(1)} %bitcast.52), channel_id=1, source_target_pairs={{0,64},{64,128},{128,192},{1,65},{65,129},{129,193},{2,66},{66,130... | collective-permute-start | bytes 196616 | tf_op jit(solution)/shard_map/ppermute | solution.py:242
  22.6 33.4 %copy-start.2 = (bf16[384,256]{1,0:T(8,128)(2,1)}, bf16[384,256]{1,0:T(8,128)(2,1)S(1)}, u32[]{:S(2)}) copy-start(bf16[384,256]{1,0:T(8,128)(2,1)S(1)} %pad_maximum_fusion) | copy-start | bytes 589828
  22.6 9.9 %collective-permute-start.4 = (bf16[384,256]{1,0:T(8,128)(2,1)S(1)}, bf16[384,256]{1,0:T(8,128)(2,1)S(1)}, u32[]{:S(2)}, u32[]{:S(2)}) collective-permute-start(bf16[384,256]{1,0:T(8,128)(2,1)S(1)} %pad_maximum_fusion), channel_id=1, source_target_pairs={{0,14},{2,0},{4,2},{6,4},{8,6},{10,8},{12,10},{14,12},{1,15},{3,1}... | collective-permute-start | bytes 589832 | tf_op jit(solution)/shard_map/ppermute | solution.py:184
  28.5 7.7 %collective-permute-start.1 = (bf16[384,256]{1,0:T(8,128)(2,1)S(1)}, bf16[384,256]{1,0:T(8,128)(2,1)S(1)}, u32[]{:S(2)}, u32[]{:S(2)}) collective-permute-start(bf16[384,256]{1,0:T(8,128)(2,1)S(1)} %pad_maximum_fusion), channel_id=1, source_target_pairs={{0,2},{2,4},{4,6},{6,8},{8,10},{10,12},{12,14},{14,0},{1,3},{3,5},... | collective-permute-start | bytes 589832 | tf_op jit(solution)/shard_map/ppermute | solution.py:184
  32.5 6.9 %collective-permute-start.5 = (bf16[384,256]{1,0:T(8,128)(2,1)S(1)}, bf16[384,256]{1,0:T(8,128)(2,1)S(1)}, u32[]{:S(2)}, u32[]{:S(2)}) collective-permute-start(bf16[384,256]{1,0:T(8,128)(2,1)S(1)} %collective-permute-done.4), channel_id=1, source_target_pairs={{0,14},{2,0},{4,2},{6,4},{8,6},{10,8},{12,10},{14,12},{1,15},{3,1}... | collective-permute-start | bytes 589832 | tf_op jit(solution)/shard_map/ppermute | solution.py:184
  36.2 6.9 %collective-permute-start.2 = (bf16[384,256]{1,0:T(8,128)(2,1)S(1)}, bf16[384,256]{1,0:T(8,128)(2,1)S(1)}, u32[]{:S(2)}, u32[]{:S(2)}) collective-permute-start(bf16[384,256]{1,0:T(8,128)(2,1)S(1)} %collective-permute-done.1), channel_id=1, source_target_pairs={{0,2},{2,4},{4,6},{6,8},{8,10},{10,12},{12,14},{14,0},{1,3},{3,5},... | collective-permute-start | bytes 589832 | tf_op jit(solution)/shard_map/ppermute | solution.py:184
  39.4 6.9 %collective-permute-start.6 = (bf16[384,256]{1,0:T(8,128)(2,1)S(1)}, bf16[384,256]{1,0:T(8,128)(2,1)S(1)}, u32[]{:S(2)}, u32[]{:S(2)}) collective-permute-start(bf16[384,256]{1,0:T(8,128)(2,1)S(1)} %collective-permute-done.5), channel_id=1, source_target_pairs={{0,14},{2,0},{4,2},{6,4},{8,6},{10,8},{12,10},{14,12},{1,15},{3,1}... | collective-permute-start | bytes 589832 | tf_op jit(solution)/shard_map/ppermute | solution.py:184
  43.1 6.9 %collective-permute-start.3 = (bf16[384,256]{1,0:T(8,128)(2,1)S(1)}, bf16[384,256]{1,0:T(8,128)(2,1)S(1)}, u32[]{:S(2)}, u32[]{:S(2)}) collective-permute-start(bf16[384,256]{1,0:T(8,128)(2,1)S(1)} %collective-permute-done.2), channel_id=1, source_target_pairs={{0,2},{2,4},{4,6},{6,8},{8,10},{10,12},{12,14},{14,0},{1,3},{3,5},... | collective-permute-start | bytes 589832 | tf_op jit(solution)/shard_map/ppermute | solution.py:184
  50.0 4.7 %collective-permute-start.8 = (bf16[384,128]{1,0:T(8,128)(2,1)S(1)}, bf16[384,128]{1,0:T(8,128)(2,1)S(1)}, u32[]{:S(2)}, u32[]{:S(2)}) collective-permute-start(bf16[384,128]{1,0:T(8,128)(2,1)S(1)} %slice.38), channel_id=1, source_target_pairs={{0,14},{2,0},{4,2},{6,4},{8,6},{10,8},{12,10},{14,12},{1,15},{3,1}... | collective-permute-start | bytes 294920 | tf_op jit(solution)/shard_map/ppermute | solution.py:184
  50.1 5.9 %collective-permute-start.7 = (bf16[384,128]{1,0:T(8,128)(2,1)S(1)}, bf16[384,128]{1,0:T(8,128)(2,1)S(1)}, u32[]{:S(2)}, u32[]{:S(2)}) collective-permute-start(bf16[384,128]{1,0:T(8,128)(2,1)S(1)} %slice.37), channel_id=1, source_target_pairs={{0,2},{2,4},{4,6},{6,8},{8,10},{10,12},{12,14},{14,0},{1,3},{3,5},... | collective-permute-start | bytes 294920 | tf_op jit(solution)/shard_map/ppermute | solution.py:184
  68.9 6.6 %collective-permute-start.13 = (bf16[384,128]{1,0:T(8,128)(2,1)}, bf16[384,128]{1,0:T(8,128)(2,1)S(1)}, u32[]{:S(2)}, u32[]{:S(2)}) collective-permute-start(bf16[384,128]{1,0:T(8,128)(2,1)} %bitcast.54), channel_id=1, source_target_pairs={{0,14},{2,0},{4,2},{6,4},{8,6},{10,8},{12,10},{14,12},{1,15},{3,1}... | collective-permute-start | bytes 294920 | tf_op jit(solution)/shard_map/ppermute | solution.py:184
  69.4 42.3 %all-to-all-start.2 = ((bf16[8,32,4096]{2,1,0:T(8,128)(2,1)}), bf16[8,32,4096]{2,1,0:T(8,128)(2,1)S(1)}, u32[]{:S(2)}, u32[]{:S(2)}) async-start(bf16[8,32,4096]{2,1,0:T(8,128)(2,1)} %bitcast.37), calls=%async_computation.2 | async-start | bytes 4194304 | tf_op jit(solution)/shard_map/all_to_all | solution.py:188
  73.8 28.5 %copy-start.6 = (bf16[6,64,256]{2,1,0:T(8,128)(2,1)S(1)}, bf16[6,64,256]{2,1,0:T(8,128)(2,1)}, u32[]{:S(2)}) copy-start(bf16[6,64,256]{2,1,0:T(8,128)(2,1)} %get-tuple-element.26) | copy-start | bytes 589828
  73.8 6.5 %collective-permute-start.9 = (bf16[384,128]{1,0:T(8,128)(2,1)S(1)}, bf16[384,128]{1,0:T(8,128)(2,1)S(1)}, u32[]{:S(2)}, u32[]{:S(2)}) collective-permute-start(bf16[384,128]{1,0:T(8,128)(2,1)S(1)} %bitcast.53), channel_id=1, source_target_pairs={{0,2},{2,4},{4,6},{6,8},{8,10},{10,12},{12,14},{14,0},{1,3},{3,5},... | collective-permute-start | bytes 294920 | tf_op jit(solution)/shard_map/ppermute | solution.py:184
  75.6 7.1 %collective-permute-start.14 = (bf16[384,256]{1,0:T(8,128)(2,1)S(1)}, bf16[384,256]{1,0:T(8,128)(2,1)S(1)}, u32[]{:S(2)}, u32[]{:S(2)}) collective-permute-start(bf16[384,256]{1,0:T(8,128)(2,1)S(1)} %pad_maximum_fusion.2), channel_id=1, source_target_pairs={{0,14},{2,0},{4,2},{6,4},{8,6},{10,8},{12,10},{14,12},{1,15},{3,1}... | collective-permute-start | bytes 589832 | tf_op jit(solution)/shard_map/ppermute | solution.py:184
  80.4 7.8 %collective-permute-start.10 = (bf16[384,256]{1,0:T(8,128)(2,1)S(1)}, bf16[384,256]{1,0:T(8,128)(2,1)S(1)}, u32[]{:S(2)}, u32[]{:S(2)}) collective-permute-start(bf16[384,256]{1,0:T(8,128)(2,1)S(1)} %pad_maximum_fusion.1), channel_id=1, source_target_pairs={{0,2},{2,4},{4,6},{6,8},{8,10},{10,12},{12,14},{14,0},{1,3},{3,5},... | collective-permute-start | bytes 589832 | tf_op jit(solution)/shard_map/ppermute | solution.py:184
  82.8 6.6 %collective-permute-start.15 = (bf16[384,256]{1,0:T(8,128)(2,1)S(1)}, bf16[384,256]{1,0:T(8,128)(2,1)S(1)}, u32[]{:S(2)}, u32[]{:S(2)}) collective-permute-start(bf16[384,256]{1,0:T(8,128)(2,1)S(1)} %fusion), channel_id=1, source_target_pairs={{0,14},{2,0},{4,2},{6,4},{8,6},{10,8},{12,10},{14,12},{1,15},{3,1}... | collective-permute-start | bytes 589832 | tf_op jit(solution)/shard_map/ppermute | solution.py:184
  88.3 7.0 %collective-permute-start.11 = (bf16[384,256]{1,0:T(8,128)(2,1)S(1)}, bf16[384,256]{1,0:T(8,128)(2,1)S(1)}, u32[]{:S(2)}, u32[]{:S(2)}) collective-permute-start(bf16[384,256]{1,0:T(8,128)(2,1)S(1)} %fusion.2), channel_id=1, source_target_pairs={{0,2},{2,4},{4,6},{6,8},{8,10},{10,12},{12,14},{14,0},{1,3},{3,5},... | collective-permute-start | bytes 589832 | tf_op jit(solution)/shard_map/ppermute | solution.py:184
  89.5 7.0 %collective-permute-start.16 = (bf16[384,256]{1,0:T(8,128)(2,1)S(1)}, bf16[384,256]{1,0:T(8,128)(2,1)S(1)}, u32[]{:S(2)}, u32[]{:S(2)}) collective-permute-start(bf16[384,256]{1,0:T(8,128)(2,1)S(1)} %fusion.1), channel_id=1, source_target_pairs={{0,14},{2,0},{4,2},{6,4},{8,6},{10,8},{12,10},{14,12},{1,15},{3,1}... | collective-permute-start | bytes 589832 | tf_op jit(solution)/shard_map/ppermute | solution.py:184
  95.3 7.0 %collective-permute-start.12 = (bf16[384,256]{1,0:T(8,128)(2,1)S(1)}, bf16[384,256]{1,0:T(8,128)(2,1)S(1)}, u32[]{:S(2)}, u32[]{:S(2)}) collective-permute-start(bf16[384,256]{1,0:T(8,128)(2,1)S(1)} %fusion.3), channel_id=1, source_target_pairs={{0,2},{2,4},{4,6},{6,8},{8,10},{10,12},{12,14},{14,0},{1,3},{3,5},... | collective-permute-start | bytes 589832 | tf_op jit(solution)/shard_map/ppermute | solution.py:184
  102.4 8.7 %collective-permute-start.17 = (bf16[128,256]{1,0:T(8,128)(2,1)S(1)}, bf16[128,256]{1,0:T(8,128)(2,1)S(1)}, u32[]{:S(2)}, u32[]{:S(2)}) collective-permute-start(bf16[128,256]{1,0:T(8,128)(2,1)S(1)} %get-tuple-element.45), channel_id=1, source_target_pairs={{64,0},{128,64},{192,128},{65,1},{129,65},{193,129},{66,2},{130,66... | collective-permute-start | bytes 196616 | tf_op jit(solution)/shard_map/ppermute | solution.py:273
  111.7 10.2 %all-to-all-start.3 = ((bf16[8,32,256]{2,1,0:T(8,128)(2,1)}), bf16[8,32,256]{2,1,0:T(8,128)(2,1)S(1)}, u32[]{:S(2)}, u32[]{:S(2)}) async-start(bf16[8,32,256]{2,1,0:T(8,128)(2,1)} %bitcast.23), calls=%async_computation.3 | async-start | bytes 262144 | tf_op jit(solution)/shard_map/all_to_all | solution.py:188
  (18 other events, 179.7 us)
where the time goes:
time: 126 us; the launch traced here: 124 us
  starting transfers between devices  52.9 us (42%)
  waiting for transfers between devices  46.5 us (37%)
  Pallas kernels  20.7 us (16%)
  other arithmetic  1.8 us (1%)
  local copies, waits for them, and re-layouts  1.34 us (1%)
    ppermute x16, waiting for transfers between devices, around(): lax.ppermute(value, 'z', [(i, (i + step) % RING) for i in range(RING)])  34.5 us
    ppermute x16, starting transfers between devices, around(): lax.ppermute(value, 'z', [(i, (i + step) % RING) for i in range(RING)])  26.6 us
    all_to_all x4, starting transfers between devices, exchanged(): lax.all_to_all(value, HEAD_AXES, split_axis=0, concat_axis=0, tiled=True)  16.3 us
    pallas_call x1, Pallas kernels, attention(): pl.pallas_call(attention_kernel, out_shape=[big] + [jax.ShapeDtypeStruct(...  12.3 us
    all_to_all x4, waiting for transfers between devices, exchanged(): lax.all_to_all(value, HEAD_AXES, split_axis=0, concat_axis=0, tiled=True)  7.03 us
    ppermute x1, starting transfers between devices, body(): lax.ppermute(mine[:half].astype(BF16), 'y', [(i, i - 1) for i in range(1,...  6.76 us
    pallas_call x2, Pallas kernels, merge_heads(): pl.pallas_call(merge_kernel, out_shape=[whole, whole], grid=(steps,), in_...  4.19 us
    pallas_call x2, Pallas kernels, split_heads(): pl.pallas_call(split_kernel, out_shape=jax.ShapeDtypeStruct((KV_HEADS, ro...  4.17 us
  transfers between devices with their start and end apart: 22, of which 17 were waited for; matrix products, arithmetic and copies ran while one was open for 1% of the time, Pallas kernels for 4%

commit v1 on v0

--- a/solution.py
+++ b/solution.py
@@ -43,8 +43,7 @@
     v4_ref = refs[RING]
     odq_ref = refs[RING + 1]
     dkv_refs = refs[RING + 2 : 2 * RING + 2]
-    dv4_ref = refs[2 * RING + 2]
-    kwin, vwin, dwin, acc = refs[2 * RING + 3 :]
+    kwin, vwin, dwin, acc = refs[2 * RING + 2 :]
     step = pl.program_id(0)
     z = place[1]
     first = ((place[0] * ROW + step) * RING + z) * CHUNK
@@ -140,14 +139,8 @@
     def _():
         for slot in range(RING):
             whole = acc[slot]
-            keys_part = (whole[:, :, :HEAD_DIM] * SCALE).astype(BF16)
-            values_part = whole[:, :, HEAD_DIM:].astype(BF16)
-            if slot == RING // 2:
-                dkv_refs[slot][...] = keys_part
-                dv4_ref[...] = values_part
-            else:
-                dkv_refs[slot][:, :, :HEAD_DIM] = keys_part
-                dkv_refs[slot][:, :, HEAD_DIM:] = values_part
+            dkv_refs[slot][:, :, :HEAD_DIM] = (whole[:, :, :HEAD_DIM] * SCALE).astype(BF16)
+            dkv_refs[slot][:, :, HEAD_DIM:] = whole[:, :, HEAD_DIM:].astype(BF16)
 
 
 def attention(place, lengths, qdo, slots, v4):
@@ -163,12 +156,12 @@
     big = jax.ShapeDtypeStruct((ROW * CHUNK, 2 * WIDE), BF16)
     return pl.pallas_call(
         attention_kernel,
-        out_shape=[big] + [jax.ShapeDtypeStruct(shape, BF16) for shape in shapes],
+        out_shape=[big] + [jax.ShapeDtypeStruct(pair, BF16)] * RING,
         grid_spec=pltpu.PrefetchScalarGridSpec(
             num_scalar_prefetch=2,
             grid=(ROW,),
             in_specs=[rows] + kv_specs,
-            out_specs=[rows] + kv_specs,
+            out_specs=[rows] + [whole(pair)] * RING,
             scratch_shapes=[
                 pltpu.VMEM((WINDOW, HEAD_DIM), BF16),
                 pltpu.VMEM((WINDOW, HEAD_DIM), BF16),
@@ -258,14 +251,8 @@
     )
     odq = exchanged(results[0].reshape(KV_HEADS, local, 2 * WIDE))
     parts = [r.reshape(UNITS * CHUNK, -1) for r in results[1:]]
-    up = around(parts[middle], 1)
-    down = around(parts[RING], -1)
-    up = jnp.concatenate(
-        [added(parts[middle - 1][:, :HEAD_DIM], up), parts[middle - 1][:, HEAD_DIM:]], 1
-    )
-    down = jnp.concatenate(
-        [parts[middle + 1][:, :HEAD_DIM], added(parts[middle + 1][:, HEAD_DIM:], down)], 1
-    )
+    up = added(parts[middle - 1], around(parts[middle], 1))
+    down = parts[middle + 1]
     for step in range(middle - 2, 0, -1):
         up = added(parts[step], around(up, 1))
         down = added(parts[RING - step], around(down, -1))
@@ -275,7 +262,9 @@
     total = total.astype(BF16).reshape(KV_HEADS, local, 2 * HEAD_DIM)
     total, odq = lax.optimization_barrier((total, odq))
     attended, query_slope = merge_heads(odq, 2)
-    key_slope, value_slope = merge_heads(exchanged(total), 1)
+    slopes = jnp.swapaxes(exchanged(total), 0, 1)
+    key_slope = slopes[:, :, :HEAD_DIM].reshape(local, KV_HEADS * HEAD_DIM)
+    value_slope = slopes[:, :, HEAD_DIM:].reshape(local, KV_HEADS * HEAD_DIM)
     return attended, query_slope, key_slope, value_slope
 
 

time: 126 us -> 121 us (0.960); the launches traced: 124 us -> 121 us
  starting transfers between devices: 52.9 us -> 48 us
    ppermute x1, starting transfers between devices: 6.76 us -> 1.92 us  [body(): lax.ppermute(mine[:half].astype(BF16), 'y', [(i, i - 1) for i in range(1,...]
    ppermute x1, waiting for transfers between devices: 1.88 us -> 4.53 us  [body(): lax.ppermute(mine[:half].astype(BF16), 'y', [(i, i - 1) for i in range(1,...]
    pallas_call x1, Pallas kernels: 12.3 us -> 14.8 us  [attention(): pl.pallas_call(attention_kernel, out_shape=[big] + [jax.ShapeDtypeStruct(...]
    ppermute x16 -> x15, waiting for transfers between devices: 34.5 us -> 32.7 us  [around(): lax.ppermute(value, 'z', [(i, (i + step) % RING) for i in range(RING)])]
    pallas_call x2 -> x1, Pallas kernels: 4.19 us -> 2.62 us  [merge_heads(): pl.pallas_call(merge_kernel, out_shape=[whole, whole], grid=(steps,), in_...]
    ppermute x16 -> x15, starting transfers between devices: 26.6 us -> 26.6 us  [around(): lax.ppermute(value, 'z', [(i, (i + step) % RING) for i in range(RING)])]
  transfers between devices with their start and end apart: 22 -> 21, of which waited for: 17 -> 14; matrix products, arithmetic and copies ran while one was open for 1% -> 1% of each run, Pallas kernels for 4% -> 4%
where the time goes in v1:
time: 121 us
  starting transfers between devices  48 us (40%)
  waiting for transfers between devices  47.4 us (39%)
  Pallas kernels  21.6 us (18%)
  other arithmetic  1.73 us (1%)
  local copies, waits for them, and re-layouts  1.35 us (1%)
    ppermute x15, waiting for transfers between devices, around(): lax.ppermute(value, 'z', [(i, (i + step) % RING) for i in range(RING)])  32.7 us
    ppermute x15, starting transfers between devices, around(): lax.ppermute(value, 'z', [(i, (i + step) % RING) for i in range(RING)])  26.6 us
    all_to_all x4, starting transfers between devices, exchanged(): lax.all_to_all(value, HEAD_AXES, split_axis=0, concat_axis=0, tiled=True)  16.3 us
    pallas_call x1, Pallas kernels, attention(): pl.pallas_call(attention_kernel, out_shape=[big] + [jax.ShapeDtypeStruct(...  14.8 us
    all_to_all x4, waiting for transfers between devices, exchanged(): lax.all_to_all(value, HEAD_AXES, split_axis=0, concat_axis=0, tiled=True)  7.04 us
    ppermute x1, waiting for transfers between devices, body(): lax.ppermute(mine[:half].astype(BF16), 'y', [(i, i - 1) for i in range(1,...  4.53 us
    pallas_call x2, Pallas kernels, split_heads(): pl.pallas_call(split_kernel, out_shape=jax.ShapeDtypeStruct((KV_HEADS, ro...  4.16 us
    ppermute x1, starting transfers between devices, body(): lax.ppermute(own[half:], 'y', [(i, i + 1) for i in range(ROW - 1)])  3.19 us
  transfers between devices with their start and end apart: 21, of which 14 were waited for; matrix products, arithmetic and copies ran while one was open for 1% of the time, Pallas kernels for 4%

profile of v1, /device:TPU:16, one launch (start us, length us, event | category | flops | bytes accessed | tf_op | source)
XLA Modules:
  0.0 121.0 jit_solution(2151886358662812336)
XLA Ops:
  2.2 4.3 %all-to-all-start = ((bf16[8,32,256]{2,1,0:T(8,128)(2,1)}), bf16[8,32,256]{2,1,0:T(8,128)(2,1)S(1)}, u32[]{:S(2)}, u32[]{:S(2)}) async-start(bf16[8,32,256]{2,1,0:T(8,128)(2,1)} %shard_map.84), calls=%async_computation | async-start | bytes 262144 | tf_op jit(solution)/shard_map/all_to_all | solution.py:181
  9.1 3.5 %all-to-all-done = bf16[8,32,256]{2,1,0:T(8,128)(2,1)S(1)} async-done(((bf16[8,32,256]{2,1,0:T(8,128)(2,1)}), bf16[8,32,256]{2,1,0:T(8,128)(2,1)S(1)}, u32[]{:S(2)}, u32[]{:S(2)}) %all-to-all-start) | async-done | bytes 131104 | tf_op jit(solution)/shard_map/all_to_all | solution.py:181
  12.6 3.6 %all-to-all-start.1 = ((bf16[8,32,4096]{2,1,0:T(8,128)(2,1)}), bf16[8,32,4096]{2,1,0:T(8,128)(2,1)S(1)}, u32[]{:S(2)}, u32[]{:S(2)}) async-start(bf16[8,32,4096]{2,1,0:T(8,128)(2,1)} %shard_map.85), calls=%async_computation.1 | async-start | bytes 4194304 | tf_op jit(solution)/shard_map/all_to_all | solution.py:181
  16.2 3.2 %collective-permute-start = (bf16[128,256]{1,0:T(8,128)(2,1)S(1)}, bf16[128,256]{1,0:T(8,128)(2,1)S(1)}, u32[]{:S(2)}, u32[]{:S(2)}) collective-permute-start(bf16[128,256]{1,0:T(8,128)(2,1)S(1)} %bitcast.59), channel_id=1, source_target_pairs={{0,64},{64,128},{128,192},{1,65},{65,129},{129,193},{2,66},{66,130... | collective-permute-start | bytes 196616 | tf_op jit(solution)/shard_map/ppermute | solution.py:235
  19.4 3.1 %collective-permute-done = bf16[128,256]{1,0:T(8,128)(2,1)S(1)} collective-permute-done((bf16[128,256]{1,0:T(8,128)(2,1)S(1)}, bf16[128,256]{1,0:T(8,128)(2,1)S(1)}, u32[]{:S(2)}, u32[]{:S(2)}) %collective-permute-start) | collective-permute-done | bytes 65568 | tf_op jit(solution)/shard_map/ppermute | solution.py:235
  22.6 5.9 %collective-permute-start.4 = (bf16[384,256]{1,0:T(8,128)(2,1)S(1)}, bf16[384,256]{1,0:T(8,128)(2,1)S(1)}, u32[]{:S(2)}, u32[]{:S(2)}) collective-permute-start(bf16[384,256]{1,0:T(8,128)(2,1)S(1)} %pad_maximum_fusion), channel_id=1, source_target_pairs={{0,14},{2,0},{4,2},{6,4},{8,6},{10,8},{12,10},{14,12},{1,15},{3,1}... | collective-permute-start | bytes 589832 | tf_op jit(solution)/shard_map/ppermute | solution.py:177
  28.5 4.0 %collective-permute-done.4 = bf16[384,256]{1,0:T(8,128)(2,1)S(1)} collective-permute-done((bf16[384,256]{1,0:T(8,128)(2,1)S(1)}, bf16[384,256]{1,0:T(8,128)(2,1)S(1)}, u32[]{:S(2)}, u32[]{:S(2)}) %collective-permute-start.4) | collective-permute-done | bytes 196640 | tf_op jit(solution)/shard_map/ppermute | solution.py:177
  32.5 3.7 %collective-permute-start.5 = (bf16[384,256]{1,0:T(8,128)(2,1)S(1)}, bf16[384,256]{1,0:T(8,128)(2,1)S(1)}, u32[]{:S(2)}, u32[]{:S(2)}) collective-permute-start(bf16[384,256]{1,0:T(8,128)(2,1)S(1)} %collective-permute-done.4), channel_id=1, source_target_pairs={{0,14},{2,0},{4,2},{6,4},{8,6},{10,8},{12,10},{14,12},{1,15},{3,1}... | collective-permute-start | bytes 589832 | tf_op jit(solution)/shard_map/ppermute | solution.py:177
  36.2 3.2 %collective-permute-done.5 = bf16[384,256]{1,0:T(8,128)(2,1)S(1)} collective-permute-done((bf16[384,256]{1,0:T(8,128)(2,1)S(1)}, bf16[384,256]{1,0:T(8,128)(2,1)S(1)}, u32[]{:S(2)}, u32[]{:S(2)}) %collective-permute-start.5) | collective-permute-done | bytes 196640 | tf_op jit(solution)/shard_map/ppermute | solution.py:177
  39.4 3.7 %collective-permute-start.6 = (bf16[384,256]{1,0:T(8,128)(2,1)S(1)}, bf16[384,256]{1,0:T(8,128)(2,1)S(1)}, u32[]{:S(2)}, u32[]{:S(2)}) collective-permute-start(bf16[384,256]{1,0:T(8,128)(2,1)S(1)} %collective-permute-done.5), channel_id=1, source_target_pairs={{0,14},{2,0},{4,2},{6,4},{8,6},{10,8},{12,10},{14,12},{1,15},{3,1}... | collective-permute-start | bytes 589832 | tf_op jit(solution)/shard_map/ppermute | solution.py:177
  43.1 3.2 %collective-permute-done.6 = bf16[384,256]{1,0:T(8,128)(2,1)S(1)} collective-permute-done((bf16[384,256]{1,0:T(8,128)(2,1)S(1)}, bf16[384,256]{1,0:T(8,128)(2,1)S(1)}, u32[]{:S(2)}, u32[]{:S(2)}) %collective-permute-start.6) | collective-permute-done | bytes 196640 | tf_op jit(solution)/shard_map/ppermute | solution.py:177
  46.3 3.7 %collective-permute-done.3 = bf16[384,256]{1,0:T(8,128)(2,1)S(1)} collective-permute-done((bf16[384,256]{1,0:T(8,128)(2,1)S(1)}, bf16[384,256]{1,0:T(8,128)(2,1)S(1)}, u32[]{:S(2)}, u32[]{:S(2)}) %collective-permute-start.3) | collective-permute-done | bytes 196640 | tf_op jit(solution)/shard_map/ppermute | solution.py:177
  56.6 14.8 %shard_map.86 = (bf16[256,4096]{1,0:T(8,128)(2,1)}, bf16[6,64,256]{2,1,0:T(8,128)(2,1)}, bf16[6,64,256]{2,1,0:T(8,128)(2,1)}, bf16[6,64,256]{2,1,0:T(8,128)(2,1)...) custom-call(s32[2]{0:T(128)} %pad_add_fusion.place, ...), custom_call_target="tpu_custom_call" | custom-call | tf_op jit(solution)/shard_map/pallas_call | solution.py:157
  71.6 4.4 %all-to-all-start.2 = ((bf16[8,32,4096]{2,1,0:T(8,128)(2,1)}), bf16[8,32,4096]{2,1,0:T(8,128)(2,1)S(1)}, u32[]{:S(2)}, u32[]{:S(2)}) async-start(bf16[8,32,4096]{2,1,0:T(8,128)(2,1)} %bitcast.47), calls=%async_computation.2 | async-start | bytes 4194304 | tf_op jit(solution)/shard_map/all_to_all | solution.py:181
  76.0 3.3 %collective-permute-start.13 = (bf16[384,256]{1,0:T(8,128)(2,1)S(1)}, bf16[384,256]{1,0:T(8,128)(2,1)S(1)}, u32[]{:S(2)}, u32[]{:S(2)}) collective-permute-start(bf16[384,256]{1,0:T(8,128)(2,1)S(1)} %bitcast.60), channel_id=1, source_target_pairs={{0,14},{2,0},{4,2},{6,4},{8,6},{10,8},{12,10},{14,12},{1,15},{3,1}... | collective-permute-start | bytes 589832 | tf_op jit(solution)/shard_map/ppermute | solution.py:177
  79.4 4.7 %collective-permute-done.13 = bf16[384,256]{1,0:T(8,128)(2,1)S(1)} collective-permute-done((bf16[384,256]{1,0:T(8,128)(2,1)S(1)}, bf16[384,256]{1,0:T(8,128)(2,1)S(1)}, u32[]{:S(2)}, u32[]{:S(2)}) %collective-permute-start.13) | collective-permute-done | bytes 196640 | tf_op jit(solution)/shard_map/ppermute | solution.py:177
  84.2 3.8 %collective-permute-start.14 = (bf16[384,256]{1,0:T(8,128)(2,1)S(1)}, bf16[384,256]{1,0:T(8,128)(2,1)S(1)}, u32[]{:S(2)}, u32[]{:S(2)}) collective-permute-start(bf16[384,256]{1,0:T(8,128)(2,1)S(1)} %fusion), channel_id=1, source_target_pairs={{0,14},{2,0},{4,2},{6,4},{8,6},{10,8},{12,10},{14,12},{1,15},{3,1}... | collective-permute-start | bytes 589832 | tf_op jit(solution)/shard_map/ppermute | solution.py:177
  88.1 3.9 %collective-permute-done.14 = bf16[384,256]{1,0:T(8,128)(2,1)S(1)} collective-permute-done((bf16[384,256]{1,0:T(8,128)(2,1)S(1)}, bf16[384,256]{1,0:T(8,128)(2,1)S(1)}, u32[]{:S(2)}, u32[]{:S(2)}) %collective-permute-start.14) | collective-permute-done | bytes 196640 | tf_op jit(solution)/shard_map/ppermute | solution.py:177
  92.0 3.8 %collective-permute-start.15 = (bf16[384,256]{1,0:T(8,128)(2,1)S(1)}, bf16[384,256]{1,0:T(8,128)(2,1)S(1)}, u32[]{:S(2)}, u32[]{:S(2)}) collective-permute-start(bf16[384,256]{1,0:T(8,128)(2,1)S(1)} %fusion.1), channel_id=1, source_target_pairs={{0,14},{2,0},{4,2},{6,4},{8,6},{10,8},{12,10},{14,12},{1,15},{3,1}... | collective-permute-start | bytes 589832 | tf_op jit(solution)/shard_map/ppermute | solution.py:177
  96.0 3.0 %collective-permute-done.15 = bf16[384,256]{1,0:T(8,128)(2,1)S(1)} collective-permute-done((bf16[384,256]{1,0:T(8,128)(2,1)S(1)}, bf16[384,256]{1,0:T(8,128)(2,1)S(1)}, u32[]{:S(2)}, u32[]{:S(2)}) %collective-permute-start.15) | collective-permute-done | bytes 196640 | tf_op jit(solution)/shard_map/ppermute | solution.py:177
  99.0 3.8 %collective-permute-done.12 = bf16[384,256]{1,0:T(8,128)(2,1)S(1)} collective-permute-done((bf16[384,256]{1,0:T(8,128)(2,1)S(1)}, bf16[384,256]{1,0:T(8,128)(2,1)S(1)}, u32[]{:S(2)}, u32[]{:S(2)}) %collective-permute-start.12) | collective-permute-done | bytes 196640 | tf_op jit(solution)/shard_map/ppermute | solution.py:177
  104.9 4.5 %collective-permute-done.16 = bf16[128,256]{1,0:T(8,128)(2,1)S(1)} collective-permute-done((bf16[128,256]{1,0:T(8,128)(2,1)S(1)}, bf16[128,256]{1,0:T(8,128)(2,1)S(1)}, u32[]{:S(2)}, u32[]{:S(2)}) %collective-permute-start.16) | collective-permute-done | bytes 65568 | tf_op jit(solution)/shard_map/ppermute | solution.py:260
  110.1 4.1 %all-to-all-start.3 = ((bf16[8,32,256]{2,1,0:T(8,128)(2,1)}), bf16[8,32,256]{2,1,0:T(8,128)(2,1)S(1)}, u32[]{:S(2)}, u32[]{:S(2)}) async-start(bf16[8,32,256]{2,1,0:T(8,128)(2,1)} %bitcast.22), calls=%async_computation.3 | async-start | bytes 262144 | tf_op jit(solution)/shard_map/all_to_all | solution.py:181
  116.8 3.5 %all-to-all-done.3 = bf16[8,32,256]{2,1,0:T(8,128)(2,1)S(1)} async-done(((bf16[8,32,256]{2,1,0:T(8,128)(2,1)}), bf16[8,32,256]{2,1,0:T(8,128)(2,1)S(1)}, u32[]{:S(2)}, u32[]{:S(2)}) %all-to-all-start.3) | async-done | bytes 131104 | tf_op jit(solution)/shard_map/all_to_all | solution.py:181
  (74 shorter events, 17.5 us)
Async XLA Ops:
  2.2 10.4 %all-to-all-start = ((bf16[8,32,256]{2,1,0:T(8,128)(2,1)}), bf16[8,32,256]{2,1,0:T(8,128)(2,1)S(1)}, u32[]{:S(2)}, u32[]{:S(2)}) async-start(bf16[8,32,256]{2,1,0:T(8,128)(2,1)} %shard_map.84), calls=%async_computation | async-start | bytes 262144 | tf_op jit(solution)/shard_map/all_to_all | solution.py:181
  12.6 37.3 %all-to-all-start.1 = ((bf16[8,32,4096]{2,1,0:T(8,128)(2,1)}), bf16[8,32,4096]{2,1,0:T(8,128)(2,1)S(1)}, u32[]{:S(2)}, u32[]{:S(2)}) async-start(bf16[8,32,4096]{2,1,0:T(8,128)(2,1)} %shard_map.85), calls=%async_computation.1 | async-start | bytes 4194304 | tf_op jit(solution)/shard_map/all_to_all | solution.py:181
  16.2 6.3 %collective-permute-start = (bf16[128,256]{1,0:T(8,128)(2,1)S(1)}, bf16[128,256]{1,0:T(8,128)(2,1)S(1)}, u32[]{:S(2)}, u32[]{:S(2)}) collective-permute-start(bf16[128,256]{1,0:T(8,128)(2,1)S(1)} %bitcast.59), channel_id=1, source_target_pairs={{0,64},{64,128},{128,192},{1,65},{65,129},{129,193},{2,66},{66,130... | collective-permute-start | bytes 196616 | tf_op jit(solution)/shard_map/ppermute | solution.py:235
  22.6 33.4 %copy-start.2 = (bf16[384,256]{1,0:T(8,128)(2,1)}, bf16[384,256]{1,0:T(8,128)(2,1)S(1)}, u32[]{:S(2)}) copy-start(bf16[384,256]{1,0:T(8,128)(2,1)S(1)} %pad_maximum_fusion) | copy-start | bytes 589828
  22.6 9.9 %collective-permute-start.4 = (bf16[384,256]{1,0:T(8,128)(2,1)S(1)}, bf16[384,256]{1,0:T(8,128)(2,1)S(1)}, u32[]{:S(2)}, u32[]{:S(2)}) collective-permute-start(bf16[384,256]{1,0:T(8,128)(2,1)S(1)} %pad_maximum_fusion), channel_id=1, source_target_pairs={{0,14},{2,0},{4,2},{6,4},{8,6},{10,8},{12,10},{14,12},{1,15},{3,1}... | collective-permute-start | bytes 589832 | tf_op jit(solution)/shard_map/ppermute | solution.py:177
  28.5 7.7 %collective-permute-start.1 = (bf16[384,256]{1,0:T(8,128)(2,1)S(1)}, bf16[384,256]{1,0:T(8,128)(2,1)S(1)}, u32[]{:S(2)}, u32[]{:S(2)}) collective-permute-start(bf16[384,256]{1,0:T(8,128)(2,1)S(1)} %pad_maximum_fusion), channel_id=1, source_target_pairs={{0,2},{2,4},{4,6},{6,8},{8,10},{10,12},{12,14},{14,0},{1,3},{3,5},... | collective-permute-start | bytes 589832 | tf_op jit(solution)/shard_map/ppermute | solution.py:177
  32.5 23.5 %copy-start.11 = (bf16[384,256]{1,0:T(8,128)(2,1)}, bf16[384,256]{1,0:T(8,128)(2,1)S(1)}, u32[]{:S(2)}) copy-start(bf16[384,256]{1,0:T(8,128)(2,1)S(1)} %collective-permute-done.4) | copy-start | bytes 589828
  32.5 6.9 %collective-permute-start.5 = (bf16[384,256]{1,0:T(8,128)(2,1)S(1)}, bf16[384,256]{1,0:T(8,128)(2,1)S(1)}, u32[]{:S(2)}, u32[]{:S(2)}) collective-permute-start(bf16[384,256]{1,0:T(8,128)(2,1)S(1)} %collective-permute-done.4), channel_id=1, source_target_pairs={{0,14},{2,0},{4,2},{6,4},{8,6},{10,8},{12,10},{14,12},{1,15},{3,1}... | collective-permute-start | bytes 589832 | tf_op jit(solution)/shard_map/ppermute | solution.py:177
  36.2 6.9 %collective-permute-start.2 = (bf16[384,256]{1,0:T(8,128)(2,1)S(1)}, bf16[384,256]{1,0:T(8,128)(2,1)S(1)}, u32[]{:S(2)}, u32[]{:S(2)}) collective-permute-start(bf16[384,256]{1,0:T(8,128)(2,1)S(1)} %collective-permute-done.1), channel_id=1, source_target_pairs={{0,2},{2,4},{4,6},{6,8},{8,10},{10,12},{12,14},{14,0},{1,3},{3,5},... | collective-permute-start | bytes 589832 | tf_op jit(solution)/shard_map/ppermute | solution.py:177
  39.4 6.9 %collective-permute-start.6 = (bf16[384,256]{1,0:T(8,128)(2,1)S(1)}, bf16[384,256]{1,0:T(8,128)(2,1)S(1)}, u32[]{:S(2)}, u32[]{:S(2)}) collective-permute-start(bf16[384,256]{1,0:T(8,128)(2,1)S(1)} %collective-permute-done.5), channel_id=1, source_target_pairs={{0,14},{2,0},{4,2},{6,4},{8,6},{10,8},{12,10},{14,12},{1,15},{3,1}... | collective-permute-start | bytes 589832 | tf_op jit(solution)/shard_map/ppermute | solution.py:177
  43.1 6.9 %collective-permute-start.3 = (bf16[384,256]{1,0:T(8,128)(2,1)S(1)}, bf16[384,256]{1,0:T(8,128)(2,1)S(1)}, u32[]{:S(2)}, u32[]{:S(2)}) collective-permute-start(bf16[384,256]{1,0:T(8,128)(2,1)S(1)} %collective-permute-done.2), channel_id=1, source_target_pairs={{0,2},{2,4},{4,6},{6,8},{8,10},{10,12},{12,14},{14,0},{1,3},{3,5},... | collective-permute-start | bytes 589832 | tf_op jit(solution)/shard_map/ppermute | solution.py:177
  50.0 4.7 %collective-permute-start.8 = (bf16[384,128]{1,0:T(8,128)(2,1)S(1)}, bf16[384,128]{1,0:T(8,128)(2,1)S(1)}, u32[]{:S(2)}, u32[]{:S(2)}) collective-permute-start(bf16[384,128]{1,0:T(8,128)(2,1)S(1)} %slice.32), channel_id=1, source_target_pairs={{0,14},{2,0},{4,2},{6,4},{8,6},{10,8},{12,10},{14,12},{1,15},{3,1}... | collective-permute-start | bytes 294920 | tf_op jit(solution)/shard_map/ppermute | solution.py:177
  50.1 5.9 %collective-permute-start.7 = (bf16[384,128]{1,0:T(8,128)(2,1)S(1)}, bf16[384,128]{1,0:T(8,128)(2,1)S(1)}, u32[]{:S(2)}, u32[]{:S(2)}) collective-permute-start(bf16[384,128]{1,0:T(8,128)(2,1)S(1)} %slice.31), channel_id=1, source_target_pairs={{0,2},{2,4},{4,6},{6,8},{8,10},{10,12},{12,14},{14,0},{1,3},{3,5},... | collective-permute-start | bytes 294920 | tf_op jit(solution)/shard_map/ppermute | solution.py:177
  71.5 7.8 %collective-permute-start.9 = (bf16[384,256]{1,0:T(8,128)(2,1)}, bf16[384,256]{1,0:T(8,128)(2,1)S(1)}, u32[]{:S(2)}, u32[]{:S(2)}) collective-permute-start(bf16[384,256]{1,0:T(8,128)(2,1)} %bitcast.61), channel_id=1, source_target_pairs={{0,2},{2,4},{4,6},{6,8},{8,10},{10,12},{12,14},{14,0},{1,3},{3,5},... | collective-permute-start | bytes 589832 | tf_op jit(solution)/shard_map/ppermute | solution.py:177
  71.6 38.5 %all-to-all-start.2 = ((bf16[8,32,4096]{2,1,0:T(8,128)(2,1)}), bf16[8,32,4096]{2,1,0:T(8,128)(2,1)S(1)}, u32[]{:S(2)}, u32[]{:S(2)}) async-start(bf16[8,32,4096]{2,1,0:T(8,128)(2,1)} %bitcast.47), calls=%async_computation.2 | async-start | bytes 4194304 | tf_op jit(solution)/shard_map/all_to_all | solution.py:181
  76.0 26.9 %copy-start.5 = (bf16[6,64,256]{2,1,0:T(8,128)(2,1)S(1)}, bf16[6,64,256]{2,1,0:T(8,128)(2,1)}, u32[]{:S(2)}) copy-start(bf16[6,64,256]{2,1,0:T(8,128)(2,1)} %get-tuple-element.23) | copy-start | bytes 589828
  76.0 8.1 %collective-permute-start.13 = (bf16[384,256]{1,0:T(8,128)(2,1)S(1)}, bf16[384,256]{1,0:T(8,128)(2,1)S(1)}, u32[]{:S(2)}, u32[]{:S(2)}) collective-permute-start(bf16[384,256]{1,0:T(8,128)(2,1)S(1)} %bitcast.60), channel_id=1, source_target_pairs={{0,14},{2,0},{4,2},{6,4},{8,6},{10,8},{12,10},{14,12},{1,15},{3,1}... | collective-permute-start | bytes 589832 | tf_op jit(solution)/shard_map/ppermute | solution.py:177
  79.3 8.6 %collective-permute-start.10 = (bf16[384,256]{1,0:T(8,128)(2,1)S(1)}, bf16[384,256]{1,0:T(8,128)(2,1)S(1)}, u32[]{:S(2)}, u32[]{:S(2)}) collective-permute-start(bf16[384,256]{1,0:T(8,128)(2,1)S(1)} %fusion.2), channel_id=1, source_target_pairs={{0,2},{2,4},{4,6},{6,8},{8,10},{10,12},{12,14},{14,0},{1,3},{3,5},... | collective-permute-start | bytes 589832 | tf_op jit(solution)/shard_map/ppermute | solution.py:177
  84.2 7.8 %collective-permute-start.14 = (bf16[384,256]{1,0:T(8,128)(2,1)S(1)}, bf16[384,256]{1,0:T(8,128)(2,1)S(1)}, u32[]{:S(2)}, u32[]{:S(2)}) collective-permute-start(bf16[384,256]{1,0:T(8,128)(2,1)S(1)} %fusion), channel_id=1, source_target_pairs={{0,14},{2,0},{4,2},{6,4},{8,6},{10,8},{12,10},{14,12},{1,15},{3,1}... | collective-permute-start | bytes 589832 | tf_op jit(solution)/shard_map/ppermute | solution.py:177
  88.0 7.8 %collective-permute-start.11 = (bf16[384,256]{1,0:T(8,128)(2,1)S(1)}, bf16[384,256]{1,0:T(8,128)(2,1)S(1)}, u32[]{:S(2)}, u32[]{:S(2)}) collective-permute-start(bf16[384,256]{1,0:T(8,128)(2,1)S(1)} %fusion.3), channel_id=1, source_target_pairs={{0,2},{2,4},{4,6},{6,8},{8,10},{10,12},{12,14},{14,0},{1,3},{3,5},... | collective-permute-start | bytes 589832 | tf_op jit(solution)/shard_map/ppermute | solution.py:177
  92.0 7.0 %collective-permute-start.15 = (bf16[384,256]{1,0:T(8,128)(2,1)S(1)}, bf16[384,256]{1,0:T(8,128)(2,1)S(1)}, u32[]{:S(2)}, u32[]{:S(2)}) collective-permute-start(bf16[384,256]{1,0:T(8,128)(2,1)S(1)} %fusion.1), channel_id=1, source_target_pairs={{0,14},{2,0},{4,2},{6,4},{8,6},{10,8},{12,10},{14,12},{1,15},{3,1}... | collective-permute-start | bytes 589832 | tf_op jit(solution)/shard_map/ppermute | solution.py:177
  95.9 7.0 %collective-permute-start.12 = (bf16[384,256]{1,0:T(8,128)(2,1)S(1)}, bf16[384,256]{1,0:T(8,128)(2,1)S(1)}, u32[]{:S(2)}, u32[]{:S(2)}) collective-permute-start(bf16[384,256]{1,0:T(8,128)(2,1)S(1)} %fusion.4), channel_id=1, source_target_pairs={{0,2},{2,4},{4,6},{6,8},{8,10},{10,12},{12,14},{14,0},{1,3},{3,5},... | collective-permute-start | bytes 589832 | tf_op jit(solution)/shard_map/ppermute | solution.py:177
  103.0 6.5 %collective-permute-start.16 = (bf16[128,256]{1,0:T(8,128)(2,1)S(1)}, bf16[128,256]{1,0:T(8,128)(2,1)S(1)}, u32[]{:S(2)}, u32[]{:S(2)}) collective-permute-start(bf16[128,256]{1,0:T(8,128)(2,1)S(1)} %get-tuple-element.39), channel_id=1, source_target_pairs={{64,0},{128,64},{192,128},{65,1},{129,65},{193,129},{66,2},{130,66... | collective-permute-start | bytes 196616 | tf_op jit(solution)/shard_map/ppermute | solution.py:260
  110.1 10.2 %all-to-all-start.3 = ((bf16[8,32,256]{2,1,0:T(8,128)(2,1)}), bf16[8,32,256]{2,1,0:T(8,128)(2,1)S(1)}, u32[]{:S(2)}, u32[]{:S(2)}) async-start(bf16[8,32,256]{2,1,0:T(8,128)(2,1)} %bitcast.22), calls=%async_computation.3 | async-start | bytes 262144 | tf_op jit(solution)/shard_map/all_to_all | solution.py:181
  (15 other events, 158.6 us)

commit v2 on v1

--- a/solution.py
+++ b/solution.py
@@ -18,7 +18,7 @@
 UNITS = ROW + 2
 REACH = 16
 WINDOW = (REACH + 1) * CHUNK
-CLASSES = (17, 13, 11, 9, 7, 5, 3)
+CLASSES = (17, 14, 12, 10, 8, 6, 4)
 HEADS_STEP = 16
 ROWS_STEP = HEADS_STEP * CHUNK
 MASK_FILL = -1e30
@@ -82,8 +82,6 @@
         columns = base + skipped * CHUNK + lax.broadcasted_iota(jnp.int32, (CHUNK, width), 1)
         allowed = (columns >= starts) & (columns <= tokens)
         bias = jnp.where(allowed, 0.0, MASK_FILL).astype(F32)[None]
-        dwin[:, :width] = jnp.zeros((2 * HEAD_DIM, width), F32)
-
         def block(number, carry):
             lanes = pl.multiple_of(number * (HEADS_STEP * HEAD_DIM), HEADS_STEP * HEAD_DIM)
             span = pl.ds(lanes, HEADS_STEP * HEAD_DIM)
@@ -117,11 +115,11 @@
             slopes = (probabilities * (dot_t(do, values) - delta)).astype(BF16)
             odq_ref[:, span] = unstack(attended)
             odq_ref[:, other] = unstack((dot(slopes, keys) * SCALE).astype(BF16))
-            dwin[:HEAD_DIM, :width] += dot(q.astype(F32).T.astype(BF16), slopes)
-            dwin[HEAD_DIM:, :width] += dot(do.astype(F32).T.astype(BF16), weights)
+            dwin[:HEAD_DIM, :width] = dot(q.astype(F32).T.astype(BF16), slopes)
+            dwin[HEAD_DIM:, :width] = dot(do.astype(F32).T.astype(BF16), weights)
             return carry
 
-        lax.fori_loop(0, GROUP // HEADS_STEP, block, 0)
+        block(0, 0)
         back = dwin[:, :width].T
         for t in range(skipped, REACH + 1):
             at = (t - skipped) * CHUNK

time: 121 us -> 122 us (level)
  the two profiles are of different devices: /device:TPU:16 before, /device:TPU:1 now
where the time goes in v2:
time: 122 us
  starting transfers between devices  55.6 us (46%)
  waiting for transfers between devices  39.4 us (32%)
  Pallas kernels  22.9 us (19%)
  other arithmetic  1.73 us (1%)
  local copies, waits for them, and re-layouts  1.35 us (1%)
    ppermute x15, waiting for transfers between devices, around(): lax.ppermute(value, 'z', [(i, (i + step) % RING) for i in range(RING)])  29 us
    ppermute x15, starting transfers between devices, around(): lax.ppermute(value, 'z', [(i, (i + step) % RING) for i in range(RING)])  26.1 us
    all_to_all x4, starting transfers between devices, exchanged(): lax.all_to_all(value, HEAD_AXES, split_axis=0, concat_axis=0, tiled=True)  25.6 us
    pallas_call x1, Pallas kernels, attention(): pl.pallas_call(attention_kernel, out_shape=[big] + [jax.ShapeDtypeStruct(...  16.1 us
    all_to_all x4, waiting for transfers between devices, exchanged(): lax.all_to_all(value, HEAD_AXES, split_axis=0, concat_axis=0, tiled=True)  5.35 us
    pallas_call x2, Pallas kernels, split_heads(): pl.pallas_call(split_kernel, out_shape=jax.ShapeDtypeStruct((KV_HEADS, ro...  4.16 us
    ppermute x1, waiting for transfers between devices, body(): lax.ppermute(mine[:half].astype(BF16), 'y', [(i, i - 1) for i in range(1,...  3.71 us
    pallas_call x1, Pallas kernels, merge_heads(): pl.pallas_call(merge_kernel, out_shape=[whole, whole], grid=(steps,), in_...  2.61 us
  transfers between devices with their start and end apart: 21, of which 14 were waited for; matrix products, arithmetic and copies ran while one was open for 1% of the time, Pallas kernels for 4%

profile of v2, /device:TPU:1, one launch (start us, length us, event | category | flops | bytes accessed | tf_op | source)
XLA Modules:
  0.0 121.8 jit_solution(18118056718504671085)
XLA Ops:
  2.2 6.5 %all-to-all-start = ((bf16[8,32,256]{2,1,0:T(8,128)(2,1)}), bf16[8,32,256]{2,1,0:T(8,128)(2,1)S(1)}, u32[]{:S(2)}, u32[]{:S(2)}) async-start(bf16[8,32,256]{2,1,0:T(8,128)(2,1)} %shard_map.84), calls=%async_computation | async-start | bytes 262144 | tf_op jit(solution)/shard_map/all_to_all | solution.py:179
  8.7 2.6 %shard_map.85 = bf16[8,32,4096]{2,1,0:T(8,128)(2,1)} custom-call(bf16[32,16384]{1,0:T(8,128)(2,1)} %a_ref.3, bf16[32,16384]{1,0:T(8,128)(2,1)} %b_ref.3), custom_call_target="tpu_custom_call" | custom-call | tf_op jit(solution)/shard_map/pallas_call | solution.py:193
  11.3 2.7 %all-to-all-done = bf16[8,32,256]{2,1,0:T(8,128)(2,1)S(1)} async-done(((bf16[8,32,256]{2,1,0:T(8,128)(2,1)}), bf16[8,32,256]{2,1,0:T(8,128)(2,1)S(1)}, u32[]{:S(2)}, u32[]{:S(2)}) %all-to-all-start) | async-done | bytes 131104 | tf_op jit(solution)/shard_map/all_to_all | solution.py:179
  14.0 4.4 %all-to-all-start.1 = ((bf16[8,32,4096]{2,1,0:T(8,128)(2,1)}), bf16[8,32,4096]{2,1,0:T(8,128)(2,1)S(1)}, u32[]{:S(2)}, u32[]{:S(2)}) async-start(bf16[8,32,4096]{2,1,0:T(8,128)(2,1)} %shard_map.85), calls=%async_computation.1 | async-start | bytes 4194304 | tf_op jit(solution)/shard_map/all_to_all | solution.py:179
  22.2 5.7 %collective-permute-start.4 = (bf16[384,256]{1,0:T(8,128)(2,1)S(1)}, bf16[384,256]{1,0:T(8,128)(2,1)S(1)}, u32[]{:S(2)}, u32[]{:S(2)}) collective-permute-start(bf16[384,256]{1,0:T(8,128)(2,1)S(1)} %pad_maximum_fusion), channel_id=1, source_target_pairs={{0,14},{2,0},{4,2},{6,4},{8,6},{10,8},{12,10},{14,12},{1,15},{3,1}... | collective-permute-start | bytes 589832 | tf_op jit(solution)/shard_map/ppermute | solution.py:175
  27.9 3.2 %collective-permute-done.4 = bf16[384,256]{1,0:T(8,128)(2,1)S(1)} collective-permute-done((bf16[384,256]{1,0:T(8,128)(2,1)S(1)}, bf16[384,256]{1,0:T(8,128)(2,1)S(1)}, u32[]{:S(2)}, u32[]{:S(2)}) %collective-permute-start.4) | collective-permute-done | bytes 196640 | tf_op jit(solution)/shard_map/ppermute | solution.py:175
  31.1 3.4 %collective-permute-start.5 = (bf16[384,256]{1,0:T(8,128)(2,1)S(1)}, bf16[384,256]{1,0:T(8,128)(2,1)S(1)}, u32[]{:S(2)}, u32[]{:S(2)}) collective-permute-start(bf16[384,256]{1,0:T(8,128)(2,1)S(1)} %collective-permute-done.4), channel_id=1, source_target_pairs={{0,14},{2,0},{4,2},{6,4},{8,6},{10,8},{12,10},{14,12},{1,15},{3,1}... | collective-permute-start | bytes 589832 | tf_op jit(solution)/shard_map/ppermute | solution.py:175
  34.5 2.6 %collective-permute-done.5 = bf16[384,256]{1,0:T(8,128)(2,1)S(1)} collective-permute-done((bf16[384,256]{1,0:T(8,128)(2,1)S(1)}, bf16[384,256]{1,0:T(8,128)(2,1)S(1)}, u32[]{:S(2)}, u32[]{:S(2)}) %collective-permute-start.5) | collective-permute-done | bytes 196640 | tf_op jit(solution)/shard_map/ppermute | solution.py:175
  37.1 3.4 %collective-permute-start.6 = (bf16[384,256]{1,0:T(8,128)(2,1)S(1)}, bf16[384,256]{1,0:T(8,128)(2,1)S(1)}, u32[]{:S(2)}, u32[]{:S(2)}) collective-permute-start(bf16[384,256]{1,0:T(8,128)(2,1)S(1)} %collective-permute-done.5), channel_id=1, source_target_pairs={{0,14},{2,0},{4,2},{6,4},{8,6},{10,8},{12,10},{14,12},{1,15},{3,1}... | collective-permute-start | bytes 589832 | tf_op jit(solution)/shard_map/ppermute | solution.py:175
  43.2 3.1 %collective-permute-done.3 = bf16[384,256]{1,0:T(8,128)(2,1)S(1)} collective-permute-done((bf16[384,256]{1,0:T(8,128)(2,1)S(1)}, bf16[384,256]{1,0:T(8,128)(2,1)S(1)}, u32[]{:S(2)}, u32[]{:S(2)}) %collective-permute-start.3) | collective-permute-done | bytes 196640 | tf_op jit(solution)/shard_map/ppermute | solution.py:175
  46.3 3.4 %collective-permute-start.8 = (bf16[384,128]{1,0:T(8,128)(2,1)S(1)}, bf16[384,128]{1,0:T(8,128)(2,1)S(1)}, u32[]{:S(2)}, u32[]{:S(2)}) collective-permute-start(bf16[384,128]{1,0:T(8,128)(2,1)S(1)} %slice.32), channel_id=1, source_target_pairs={{0,14},{2,0},{4,2},{6,4},{8,6},{10,8},{12,10},{14,12},{1,15},{3,1}... | collective-permute-start | bytes 294920 | tf_op jit(solution)/shard_map/ppermute | solution.py:175
  51.3 3.0 %collective-permute-done.7 = bf16[384,128]{1,0:T(8,128)(2,1)S(1)} collective-permute-done((bf16[384,128]{1,0:T(8,128)(2,1)S(1)}, bf16[384,128]{1,0:T(8,128)(2,1)S(1)}, u32[]{:S(2)}, u32[]{:S(2)}) %collective-permute-start.7) | collective-permute-done | bytes 98336 | tf_op jit(solution)/shard_map/ppermute | solution.py:175
  55.0 16.1 %shard_map.86 = (bf16[256,4096]{1,0:T(8,128)(2,1)}, bf16[6,64,256]{2,1,0:T(8,128)(2,1)}, bf16[6,64,256]{2,1,0:T(8,128)(2,1)}, bf16[6,64,256]{2,1,0:T(8,128)(2,1)...) custom-call(s32[2]{0:T(128)} %pad_add_fusion.place, ...), custom_call_target="tpu_custom_call" | custom-call | tf_op jit(solution)/shard_map/pallas_call | solution.py:155
  71.2 6.7 %all-to-all-start.2 = ((bf16[8,32,4096]{2,1,0:T(8,128)(2,1)}), bf16[8,32,4096]{2,1,0:T(8,128)(2,1)S(1)}, u32[]{:S(2)}, u32[]{:S(2)}) async-start(bf16[8,32,4096]{2,1,0:T(8,128)(2,1)} %bitcast.47), calls=%async_computation.2 | async-start | bytes 4194304 | tf_op jit(solution)/shard_map/all_to_all | solution.py:179
  77.9 3.0 %collective-permute-start.13 = (bf16[384,256]{1,0:T(8,128)(2,1)S(1)}, bf16[384,256]{1,0:T(8,128)(2,1)S(1)}, u32[]{:S(2)}, u32[]{:S(2)}) collective-permute-start(bf16[384,256]{1,0:T(8,128)(2,1)S(1)} %bitcast.60), channel_id=1, source_target_pairs={{0,14},{2,0},{4,2},{6,4},{8,6},{10,8},{12,10},{14,12},{1,15},{3,1}... | collective-permute-start | bytes 589832 | tf_op jit(solution)/shard_map/ppermute | solution.py:175
  81.1 4.2 %collective-permute-done.13 = bf16[384,256]{1,0:T(8,128)(2,1)S(1)} collective-permute-done((bf16[384,256]{1,0:T(8,128)(2,1)S(1)}, bf16[384,256]{1,0:T(8,128)(2,1)S(1)}, u32[]{:S(2)}, u32[]{:S(2)}) %collective-permute-start.13) | collective-permute-done | bytes 196640 | tf_op jit(solution)/shard_map/ppermute | solution.py:175
  85.3 3.5 %collective-permute-start.14 = (bf16[384,256]{1,0:T(8,128)(2,1)S(1)}, bf16[384,256]{1,0:T(8,128)(2,1)S(1)}, u32[]{:S(2)}, u32[]{:S(2)}) collective-permute-start(bf16[384,256]{1,0:T(8,128)(2,1)S(1)} %fusion), channel_id=1, source_target_pairs={{0,14},{2,0},{4,2},{6,4},{8,6},{10,8},{12,10},{14,12},{1,15},{3,1}... | collective-permute-start | bytes 589832 | tf_op jit(solution)/shard_map/ppermute | solution.py:175
  89.0 3.3 %collective-permute-done.14 = bf16[384,256]{1,0:T(8,128)(2,1)S(1)} collective-permute-done((bf16[384,256]{1,0:T(8,128)(2,1)S(1)}, bf16[384,256]{1,0:T(8,128)(2,1)S(1)}, u32[]{:S(2)}, u32[]{:S(2)}) %collective-permute-start.14) | collective-permute-done | bytes 196640 | tf_op jit(solution)/shard_map/ppermute | solution.py:175
  92.3 3.5 %collective-permute-start.15 = (bf16[384,256]{1,0:T(8,128)(2,1)S(1)}, bf16[384,256]{1,0:T(8,128)(2,1)S(1)}, u32[]{:S(2)}, u32[]{:S(2)}) collective-permute-start(bf16[384,256]{1,0:T(8,128)(2,1)S(1)} %fusion.1), channel_id=1, source_target_pairs={{0,14},{2,0},{4,2},{6,4},{8,6},{10,8},{12,10},{14,12},{1,15},{3,1}... | collective-permute-start | bytes 589832 | tf_op jit(solution)/shard_map/ppermute | solution.py:175
  98.4 3.6 %collective-permute-done.12 = bf16[384,256]{1,0:T(8,128)(2,1)S(1)} collective-permute-done((bf16[384,256]{1,0:T(8,128)(2,1)S(1)}, bf16[384,256]{1,0:T(8,128)(2,1)S(1)}, u32[]{:S(2)}, u32[]{:S(2)}) %collective-permute-start.12) | collective-permute-done | bytes 196640 | tf_op jit(solution)/shard_map/ppermute | solution.py:175
  103.4 3.7 %collective-permute-done.16 = bf16[128,256]{1,0:T(8,128)(2,1)S(1)} collective-permute-done((bf16[128,256]{1,0:T(8,128)(2,1)S(1)}, bf16[128,256]{1,0:T(8,128)(2,1)S(1)}, u32[]{:S(2)}, u32[]{:S(2)}) %collective-permute-start.16) | collective-permute-done | bytes 65568 | tf_op jit(solution)/shard_map/ppermute | solution.py:258
  107.8 8.0 %all-to-all-start.3 = ((bf16[8,32,256]{2,1,0:T(8,128)(2,1)}), bf16[8,32,256]{2,1,0:T(8,128)(2,1)S(1)}, u32[]{:S(2)}, u32[]{:S(2)}) async-start(bf16[8,32,256]{2,1,0:T(8,128)(2,1)} %bitcast.22), calls=%async_computation.3 | async-start | bytes 262144 | tf_op jit(solution)/shard_map/all_to_all | solution.py:179
  115.8 2.6 %shard_map.87 = (bf16[32,16384]{1,0:T(8,128)(2,1)}, bf16[32,16384]{1,0:T(8,128)(2,1)}) custom-call(bf16[8,32,4096]{2,1,0:T(8,128)(2,1)} %copy-done), custom_call_target="tpu_custom_call" | custom-call | tf_op jit(solution)/shard_map/pallas_call | solution.py:214
  118.4 2.7 %all-to-all-done.3 = bf16[8,32,256]{2,1,0:T(8,128)(2,1)S(1)} async-done(((bf16[8,32,256]{2,1,0:T(8,128)(2,1)}), bf16[8,32,256]{2,1,0:T(8,128)(2,1)S(1)}, u32[]{:S(2)}, u32[]{:S(2)}) %all-to-all-start.3) | async-done | bytes 131104 | tf_op jit(solution)/shard_map/all_to_all | solution.py:179
  (74 shorter events, 16.2 us)
Async XLA Ops:
  2.2 11.8 %all-to-all-start = ((bf16[8,32,256]{2,1,0:T(8,128)(2,1)}), bf16[8,32,256]{2,1,0:T(8,128)(2,1)S(1)}, u32[]{:S(2)}, u32[]{:S(2)}) async-start(bf16[8,32,256]{2,1,0:T(8,128)(2,1)} %shard_map.84), calls=%async_computation | async-start | bytes 262144 | tf_op jit(solution)/shard_map/all_to_all | solution.py:179
  14.0 32.3 %all-to-all-start.1 = ((bf16[8,32,4096]{2,1,0:T(8,128)(2,1)}), bf16[8,32,4096]{2,1,0:T(8,128)(2,1)S(1)}, u32[]{:S(2)}, u32[]{:S(2)}) async-start(bf16[8,32,4096]{2,1,0:T(8,128)(2,1)} %shard_map.85), calls=%async_computation.1 | async-start | bytes 4194304 | tf_op jit(solution)/shard_map/all_to_all | solution.py:179
  18.4 3.8 %collective-permute-start = (bf16[128,256]{1,0:T(8,128)(2,1)S(1)}, bf16[128,256]{1,0:T(8,128)(2,1)S(1)}, u32[]{:S(2)}, u32[]{:S(2)}) collective-permute-start(bf16[128,256]{1,0:T(8,128)(2,1)S(1)} %bitcast.59), channel_id=1, source_target_pairs={{0,64},{64,128},{128,192},{1,65},{65,129},{129,193},{2,66},{66,130... | collective-permute-start | bytes 196616 | tf_op jit(solution)/shard_map/ppermute | solution.py:233
  22.2 32.1 %copy-start.2 = (bf16[384,256]{1,0:T(8,128)(2,1)}, bf16[384,256]{1,0:T(8,128)(2,1)S(1)}, u32[]{:S(2)}) copy-start(bf16[384,256]{1,0:T(8,128)(2,1)S(1)} %pad_maximum_fusion) | copy-start | bytes 589828
  22.2 8.9 %collective-permute-start.4 = (bf16[384,256]{1,0:T(8,128)(2,1)S(1)}, bf16[384,256]{1,0:T(8,128)(2,1)S(1)}, u32[]{:S(2)}, u32[]{:S(2)}) collective-permute-start(bf16[384,256]{1,0:T(8,128)(2,1)S(1)} %pad_maximum_fusion), channel_id=1, source_target_pairs={{0,14},{2,0},{4,2},{6,4},{8,6},{10,8},{12,10},{14,12},{1,15},{3,1}... | collective-permute-start | bytes 589832 | tf_op jit(solution)/shard_map/ppermute | solution.py:175
  27.9 6.6 %collective-permute-start.1 = (bf16[384,256]{1,0:T(8,128)(2,1)S(1)}, bf16[384,256]{1,0:T(8,128)(2,1)S(1)}, u32[]{:S(2)}, u32[]{:S(2)}) collective-permute-start(bf16[384,256]{1,0:T(8,128)(2,1)S(1)} %pad_maximum_fusion), channel_id=1, source_target_pairs={{0,2},{2,4},{4,6},{6,8},{8,10},{10,12},{12,14},{14,0},{1,3},{3,5},... | collective-permute-start | bytes 589832 | tf_op jit(solution)/shard_map/ppermute | solution.py:175
  31.1 23.3 %copy-start.11 = (bf16[384,256]{1,0:T(8,128)(2,1)}, bf16[384,256]{1,0:T(8,128)(2,1)S(1)}, u32[]{:S(2)}) copy-start(bf16[384,256]{1,0:T(8,128)(2,1)S(1)} %collective-permute-done.4) | copy-start | bytes 589828
  31.1 6.0 %collective-permute-start.5 = (bf16[384,256]{1,0:T(8,128)(2,1)S(1)}, bf16[384,256]{1,0:T(8,128)(2,1)S(1)}, u32[]{:S(2)}, u32[]{:S(2)}) collective-permute-start(bf16[384,256]{1,0:T(8,128)(2,1)S(1)} %collective-permute-done.4), channel_id=1, source_target_pairs={{0,14},{2,0},{4,2},{6,4},{8,6},{10,8},{12,10},{14,12},{1,15},{3,1}... | collective-permute-start | bytes 589832 | tf_op jit(solution)/shard_map/ppermute | solution.py:175
  34.5 6.0 %collective-permute-start.2 = (bf16[384,256]{1,0:T(8,128)(2,1)S(1)}, bf16[384,256]{1,0:T(8,128)(2,1)S(1)}, u32[]{:S(2)}, u32[]{:S(2)}) collective-permute-start(bf16[384,256]{1,0:T(8,128)(2,1)S(1)} %collective-permute-done.1), channel_id=1, source_target_pairs={{0,2},{2,4},{4,6},{6,8},{8,10},{10,12},{12,14},{14,0},{1,3},{3,5},... | collective-permute-start | bytes 589832 | tf_op jit(solution)/shard_map/ppermute | solution.py:175
  37.1 6.0 %collective-permute-start.6 = (bf16[384,256]{1,0:T(8,128)(2,1)S(1)}, bf16[384,256]{1,0:T(8,128)(2,1)S(1)}, u32[]{:S(2)}, u32[]{:S(2)}) collective-permute-start(bf16[384,256]{1,0:T(8,128)(2,1)S(1)} %collective-permute-done.5), channel_id=1, source_target_pairs={{0,14},{2,0},{4,2},{6,4},{8,6},{10,8},{12,10},{14,12},{1,15},{3,1}... | collective-permute-start | bytes 589832 | tf_op jit(solution)/shard_map/ppermute | solution.py:175
  40.5 5.7 %collective-permute-start.3 = (bf16[384,256]{1,0:T(8,128)(2,1)S(1)}, bf16[384,256]{1,0:T(8,128)(2,1)S(1)}, u32[]{:S(2)}, u32[]{:S(2)}) collective-permute-start(bf16[384,256]{1,0:T(8,128)(2,1)S(1)} %collective-permute-done.2), channel_id=1, source_target_pairs={{0,2},{2,4},{4,6},{6,8},{8,10},{10,12},{12,14},{14,0},{1,3},{3,5},... | collective-permute-start | bytes 589832 | tf_op jit(solution)/shard_map/ppermute | solution.py:175
  46.3 5.0 %collective-permute-start.8 = (bf16[384,128]{1,0:T(8,128)(2,1)S(1)}, bf16[384,128]{1,0:T(8,128)(2,1)S(1)}, u32[]{:S(2)}, u32[]{:S(2)}) collective-permute-start(bf16[384,128]{1,0:T(8,128)(2,1)S(1)} %slice.32), channel_id=1, source_target_pairs={{0,14},{2,0},{4,2},{6,4},{8,6},{10,8},{12,10},{14,12},{1,15},{3,1}... | collective-permute-start | bytes 294920 | tf_op jit(solution)/shard_map/ppermute | solution.py:175
  49.7 4.7 %collective-permute-start.7 = (bf16[384,128]{1,0:T(8,128)(2,1)S(1)}, bf16[384,128]{1,0:T(8,128)(2,1)S(1)}, u32[]{:S(2)}, u32[]{:S(2)}) collective-permute-start(bf16[384,128]{1,0:T(8,128)(2,1)S(1)} %slice.31), channel_id=1, source_target_pairs={{0,2},{2,4},{4,6},{6,8},{8,10},{10,12},{12,14},{14,0},{1,3},{3,5},... | collective-permute-start | bytes 294920 | tf_op jit(solution)/shard_map/ppermute | solution.py:175
  71.1 9.9 %collective-permute-start.9 = (bf16[384,256]{1,0:T(8,128)(2,1)}, bf16[384,256]{1,0:T(8,128)(2,1)S(1)}, u32[]{:S(2)}, u32[]{:S(2)}) collective-permute-start(bf16[384,256]{1,0:T(8,128)(2,1)} %bitcast.61), channel_id=1, source_target_pairs={{0,2},{2,4},{4,6},{6,8},{8,10},{10,12},{12,14},{14,0},{1,3},{3,5},... | collective-permute-start | bytes 589832 | tf_op jit(solution)/shard_map/ppermute | solution.py:175
  71.2 36.6 %all-to-all-start.2 = ((bf16[8,32,4096]{2,1,0:T(8,128)(2,1)}), bf16[8,32,4096]{2,1,0:T(8,128)(2,1)S(1)}, u32[]{:S(2)}, u32[]{:S(2)}) async-start(bf16[8,32,4096]{2,1,0:T(8,128)(2,1)} %bitcast.47), calls=%async_computation.2 | async-start | bytes 4194304 | tf_op jit(solution)/shard_map/all_to_all | solution.py:179
  77.9 24.1 %copy-start.5 = (bf16[6,64,256]{2,1,0:T(8,128)(2,1)S(1)}, bf16[6,64,256]{2,1,0:T(8,128)(2,1)}, u32[]{:S(2)}) copy-start(bf16[6,64,256]{2,1,0:T(8,128)(2,1)} %get-tuple-element.23) | copy-start | bytes 589828
  77.9 7.3 %collective-permute-start.13 = (bf16[384,256]{1,0:T(8,128)(2,1)S(1)}, bf16[384,256]{1,0:T(8,128)(2,1)S(1)}, u32[]{:S(2)}, u32[]{:S(2)}) collective-permute-start(bf16[384,256]{1,0:T(8,128)(2,1)S(1)} %bitcast.60), channel_id=1, source_target_pairs={{0,14},{2,0},{4,2},{6,4},{8,6},{10,8},{12,10},{14,12},{1,15},{3,1}... | collective-permute-start | bytes 589832 | tf_op jit(solution)/shard_map/ppermute | solution.py:175
  81.0 7.8 %collective-permute-start.10 = (bf16[384,256]{1,0:T(8,128)(2,1)S(1)}, bf16[384,256]{1,0:T(8,128)(2,1)S(1)}, u32[]{:S(2)}, u32[]{:S(2)}) collective-permute-start(bf16[384,256]{1,0:T(8,128)(2,1)S(1)} %fusion.2), channel_id=1, source_target_pairs={{0,2},{2,4},{4,6},{6,8},{8,10},{10,12},{12,14},{14,0},{1,3},{3,5},... | collective-permute-start | bytes 589832 | tf_op jit(solution)/shard_map/ppermute | solution.py:175
  85.3 6.9 %collective-permute-start.14 = (bf16[384,256]{1,0:T(8,128)(2,1)S(1)}, bf16[384,256]{1,0:T(8,128)(2,1)S(1)}, u32[]{:S(2)}, u32[]{:S(2)}) collective-permute-start(bf16[384,256]{1,0:T(8,128)(2,1)S(1)} %fusion), channel_id=1, source_target_pairs={{0,14},{2,0},{4,2},{6,4},{8,6},{10,8},{12,10},{14,12},{1,15},{3,1}... | collective-permute-start | bytes 589832 | tf_op jit(solution)/shard_map/ppermute | solution.py:175
  88.9 6.9 %collective-permute-start.11 = (bf16[384,256]{1,0:T(8,128)(2,1)S(1)}, bf16[384,256]{1,0:T(8,128)(2,1)S(1)}, u32[]{:S(2)}, u32[]{:S(2)}) collective-permute-start(bf16[384,256]{1,0:T(8,128)(2,1)S(1)} %fusion.3), channel_id=1, source_target_pairs={{0,2},{2,4},{4,6},{6,8},{8,10},{10,12},{12,14},{14,0},{1,3},{3,5},... | collective-permute-start | bytes 589832 | tf_op jit(solution)/shard_map/ppermute | solution.py:175
  92.3 6.1 %collective-permute-start.15 = (bf16[384,256]{1,0:T(8,128)(2,1)S(1)}, bf16[384,256]{1,0:T(8,128)(2,1)S(1)}, u32[]{:S(2)}, u32[]{:S(2)}) collective-permute-start(bf16[384,256]{1,0:T(8,128)(2,1)S(1)} %fusion.1), channel_id=1, source_target_pairs={{0,14},{2,0},{4,2},{6,4},{8,6},{10,8},{12,10},{14,12},{1,15},{3,1}... | collective-permute-start | bytes 589832 | tf_op jit(solution)/shard_map/ppermute | solution.py:175
  95.9 6.1 %collective-permute-start.12 = (bf16[384,256]{1,0:T(8,128)(2,1)S(1)}, bf16[384,256]{1,0:T(8,128)(2,1)S(1)}, u32[]{:S(2)}, u32[]{:S(2)}) collective-permute-start(bf16[384,256]{1,0:T(8,128)(2,1)S(1)} %fusion.4), channel_id=1, source_target_pairs={{0,2},{2,4},{4,6},{6,8},{8,10},{10,12},{12,14},{14,0},{1,3},{3,5},... | collective-permute-start | bytes 589832 | tf_op jit(solution)/shard_map/ppermute | solution.py:175
  102.1 5.0 %collective-permute-start.16 = (bf16[128,256]{1,0:T(8,128)(2,1)S(1)}, bf16[128,256]{1,0:T(8,128)(2,1)S(1)}, u32[]{:S(2)}, u32[]{:S(2)}) collective-permute-start(bf16[128,256]{1,0:T(8,128)(2,1)S(1)} %get-tuple-element.39), channel_id=1, source_target_pairs={{64,0},{128,64},{192,128},{65,1},{129,65},{193,129},{66,2},{130,66... | collective-permute-start | bytes 196616 | tf_op jit(solution)/shard_map/ppermute | solution.py:258
  107.8 13.3 %all-to-all-start.3 = ((bf16[8,32,256]{2,1,0:T(8,128)(2,1)}), bf16[8,32,256]{2,1,0:T(8,128)(2,1)S(1)}, u32[]{:S(2)}, u32[]{:S(2)}) async-start(bf16[8,32,256]{2,1,0:T(8,128)(2,1)} %bitcast.22), calls=%async_computation.3 | async-start | bytes 262144 | tf_op jit(solution)/shard_map/all_to_all | solution.py:179
  (15 other events, 177.3 us)

commit v3 on v2

--- a/solution.py
+++ b/solution.py
@@ -173,6 +173,15 @@
 
 def around(value, step):
     return lax.ppermute(value, "z", [(i, (i + step) % RING) for i in range(RING)])
+
+
+def to_earlier(value, step):
+    pairs = [
+        (y * RING + z, (y - 1) * RING + (z + step) % RING)
+        for y in range(1, ROW)
+        for z in range(RING)
+    ]
+    return lax.ppermute(value, ("y", "z"), pairs)
 
 
 def exchanged(value):
@@ -254,9 +263,13 @@
     for step in range(middle - 2, 0, -1):
         up = added(parts[step], around(up, 1))
         down = added(parts[RING - step], around(down, -1))
-    mine = parts[0].astype(F32) + around(up, 1).astype(F32) + around(down, -1).astype(F32)
-    returned = lax.ppermute(mine[:half].astype(BF16), "y", [(i, i - 1) for i in range(1, ROW)])
-    total = jnp.concatenate([mine[half : 2 * half], mine[2 * half :] + returned.astype(F32)], 0)
+    up, early = lax.optimization_barrier((up, parts[0][:half]))
+    arrivals = [lax.ppermute(early, "y", [(i, i - 1) for i in range(1, ROW)])]
+    arrivals += [to_earlier(up[:half], 1), to_earlier(down[:half], -1)]
+    total = parts[0][half:].astype(F32)
+    total = total + around(up[half:], 1).astype(F32) + around(down[half:], -1).astype(F32)
+    returned = sum(value.astype(F32) for value in arrivals)
+    total = total + jnp.pad(returned, ((half, 0), (0, 0)))
     total = total.astype(BF16).reshape(KV_HEADS, local, 2 * HEAD_DIM)
     total, odq = lax.optimization_barrier((total, odq))
     attended, query_slope = merge_heads(odq, 2)

time: 122 us -> 121 us (level)
  the two profiles are of different devices: /device:TPU:1 before, /device:TPU:16 now
where the time goes in v3:
time: 121 us; the launch traced here: 119 us
  starting transfers between devices  55.1 us (46%)
  waiting for transfers between devices  41.9 us (35%)
  Pallas kernels  18.4 us (15%)
  other arithmetic  1.7 us (1%)
  local copies, waits for them, and re-layouts  1.39 us (1%)
    ppermute x15, waiting for transfers between devices, around(): lax.ppermute(value, 'z', [(i, (i + step) % RING) for i in range(RING)])  29 us
    ppermute x15, starting transfers between devices, around(): lax.ppermute(value, 'z', [(i, (i + step) % RING) for i in range(RING)])  24.5 us
    all_to_all x4, starting transfers between devices, exchanged(): lax.all_to_all(value, HEAD_AXES, split_axis=0, concat_axis=0, tiled=True)  16.3 us
    pallas_call x1, Pallas kernels, attention(): pl.pallas_call(attention_kernel, out_shape=[big] + [jax.ShapeDtypeStruct(...  11.6 us
    ppermute x2, starting transfers between devices, to_earlier(): return lax.ppermute(value, ('y', 'z'), pairs)  9.22 us
    all_to_all x4, waiting for transfers between devices, exchanged(): lax.all_to_all(value, HEAD_AXES, split_axis=0, concat_axis=0, tiled=True)  7.04 us
    pallas_call x2, Pallas kernels, split_heads(): pl.pallas_call(split_kernel, out_shape=jax.ShapeDtypeStruct((KV_HEADS, ro...  4.16 us
    ppermute x1, starting transfers between devices, body(): lax.ppermute(own[half:], 'y', [(i, i + 1) for i in range(ROW - 1)])  3.19 us
  transfers between devices with their start and end apart: 23, of which 15 were waited for; matrix products, arithmetic and copies ran while one was open for 1% of the time, Pallas kernels for 4%

profile of v3, /device:TPU:16, one launch (start us, length us, event | category | flops | bytes accessed | tf_op | source)
XLA Modules:
  0.0 119.4 jit_solution(16392192233250695912)
XLA Ops:
  2.2 4.3 %all-to-all-start = ((bf16[8,32,256]{2,1,0:T(8,128)(2,1)}), bf16[8,32,256]{2,1,0:T(8,128)(2,1)S(1)}, u32[]{:S(2)}, u32[]{:S(2)}) async-start(bf16[8,32,256]{2,1,0:T(8,128)(2,1)} %shard_map.84), calls=%async_computation | async-start | bytes 262144 | tf_op jit(solution)/shard_map/all_to_all | solution.py:188
  6.5 2.6 %shard_map.85 = bf16[8,32,4096]{2,1,0:T(8,128)(2,1)} custom-call(bf16[32,16384]{1,0:T(8,128)(2,1)} %a_ref.3, bf16[32,16384]{1,0:T(8,128)(2,1)} %b_ref.3), custom_call_target="tpu_custom_call" | custom-call | tf_op jit(solution)/shard_map/pallas_call | solution.py:202
  9.1 3.5 %all-to-all-done = bf16[8,32,256]{2,1,0:T(8,128)(2,1)S(1)} async-done(((bf16[8,32,256]{2,1,0:T(8,128)(2,1)}), bf16[8,32,256]{2,1,0:T(8,128)(2,1)S(1)}, u32[]{:S(2)}, u32[]{:S(2)}) %all-to-all-start) | async-done | bytes 131104 | tf_op jit(solution)/shard_map/all_to_all | solution.py:188
  12.6 3.6 %all-to-all-start.1 = ((bf16[8,32,4096]{2,1,0:T(8,128)(2,1)}), bf16[8,32,4096]{2,1,0:T(8,128)(2,1)S(1)}, u32[]{:S(2)}, u32[]{:S(2)}) async-start(bf16[8,32,4096]{2,1,0:T(8,128)(2,1)} %shard_map.85), calls=%async_computation.1 | async-start | bytes 4194304 | tf_op jit(solution)/shard_map/all_to_all | solution.py:188
  16.2 3.2 %collective-permute-start = (bf16[128,256]{1,0:T(8,128)(2,1)S(1)}, bf16[128,256]{1,0:T(8,128)(2,1)S(1)}, u32[]{:S(2)}, u32[]{:S(2)}) collective-permute-start(bf16[128,256]{1,0:T(8,128)(2,1)S(1)} %bitcast.60), channel_id=1, source_target_pairs={{0,64},{64,128},{128,192},{1,65},{65,129},{129,193},{2,66},{66,130... | collective-permute-start | bytes 196616 | tf_op jit(solution)/shard_map/ppermute | solution.py:242
  19.4 3.1 %collective-permute-done = bf16[128,256]{1,0:T(8,128)(2,1)S(1)} collective-permute-done((bf16[128,256]{1,0:T(8,128)(2,1)S(1)}, bf16[128,256]{1,0:T(8,128)(2,1)S(1)}, u32[]{:S(2)}, u32[]{:S(2)}) %collective-permute-start) | collective-permute-done | bytes 65568 | tf_op jit(solution)/shard_map/ppermute | solution.py:242
  22.6 5.9 %collective-permute-start.4 = (bf16[384,256]{1,0:T(8,128)(2,1)S(1)}, bf16[384,256]{1,0:T(8,128)(2,1)S(1)}, u32[]{:S(2)}, u32[]{:S(2)}) collective-permute-start(bf16[384,256]{1,0:T(8,128)(2,1)S(1)} %pad_maximum_fusion), channel_id=1, source_target_pairs={{0,14},{2,0},{4,2},{6,4},{8,6},{10,8},{12,10},{14,12},{1,15},{3,1}... | collective-permute-start | bytes 589832 | tf_op jit(solution)/shard_map/ppermute | solution.py:175
  28.5 4.0 %collective-permute-done.4 = bf16[384,256]{1,0:T(8,128)(2,1)S(1)} collective-permute-done((bf16[384,256]{1,0:T(8,128)(2,1)S(1)}, bf16[384,256]{1,0:T(8,128)(2,1)S(1)}, u32[]{:S(2)}, u32[]{:S(2)}) %collective-permute-start.4) | collective-permute-done | bytes 196640 | tf_op jit(solution)/shard_map/ppermute | solution.py:175
  32.5 3.7 %collective-permute-start.5 = (bf16[384,256]{1,0:T(8,128)(2,1)S(1)}, bf16[384,256]{1,0:T(8,128)(2,1)S(1)}, u32[]{:S(2)}, u32[]{:S(2)}) collective-permute-start(bf16[384,256]{1,0:T(8,128)(2,1)S(1)} %collective-permute-done.4), channel_id=1, source_target_pairs={{0,14},{2,0},{4,2},{6,4},{8,6},{10,8},{12,10},{14,12},{1,15},{3,1}... | collective-permute-start | bytes 589832 | tf_op jit(solution)/shard_map/ppermute | solution.py:175
  36.2 3.2 %collective-permute-done.5 = bf16[384,256]{1,0:T(8,128)(2,1)S(1)} collective-permute-done((bf16[384,256]{1,0:T(8,128)(2,1)S(1)}, bf16[384,256]{1,0:T(8,128)(2,1)S(1)}, u32[]{:S(2)}, u32[]{:S(2)}) %collective-permute-start.5) | collective-permute-done | bytes 196640 | tf_op jit(solution)/shard_map/ppermute | solution.py:175
  39.4 3.7 %collective-permute-start.6 = (bf16[384,256]{1,0:T(8,128)(2,1)S(1)}, bf16[384,256]{1,0:T(8,128)(2,1)S(1)}, u32[]{:S(2)}, u32[]{:S(2)}) collective-permute-start(bf16[384,256]{1,0:T(8,128)(2,1)S(1)} %collective-permute-done.5), channel_id=1, source_target_pairs={{0,14},{2,0},{4,2},{6,4},{8,6},{10,8},{12,10},{14,12},{1,15},{3,1}... | collective-permute-start | bytes 589832 | tf_op jit(solution)/shard_map/ppermute | solution.py:175
  43.1 3.2 %collective-permute-done.6 = bf16[384,256]{1,0:T(8,128)(2,1)S(1)} collective-permute-done((bf16[384,256]{1,0:T(8,128)(2,1)S(1)}, bf16[384,256]{1,0:T(8,128)(2,1)S(1)}, u32[]{:S(2)}, u32[]{:S(2)}) %collective-permute-start.6) | collective-permute-done | bytes 196640 | tf_op jit(solution)/shard_map/ppermute | solution.py:175
  46.3 3.7 %collective-permute-done.3 = bf16[384,256]{1,0:T(8,128)(2,1)S(1)} collective-permute-done((bf16[384,256]{1,0:T(8,128)(2,1)S(1)}, bf16[384,256]{1,0:T(8,128)(2,1)S(1)}, u32[]{:S(2)}, u32[]{:S(2)}) %collective-permute-start.3) | collective-permute-done | bytes 196640 | tf_op jit(solution)/shard_map/ppermute | solution.py:175
  56.6 11.6 %shard_map.86 = (bf16[256,4096]{1,0:T(8,128)(2,1)}, bf16[6,64,256]{2,1,0:T(8,128)(2,1)}, bf16[6,64,256]{2,1,0:T(8,128)(2,1)}, bf16[6,64,256]{2,1,0:T(8,128)(2,1)...) custom-call(s32[2]{0:T(128)} %pad_add_fusion.place, ...), custom_call_target="tpu_custom_call" | custom-call | tf_op jit(solution)/shard_map/pallas_call | solution.py:155
  69.7 4.4 %all-to-all-start.2 = ((bf16[8,32,4096]{2,1,0:T(8,128)(2,1)}), bf16[8,32,4096]{2,1,0:T(8,128)(2,1)S(1)}, u32[]{:S(2)}, u32[]{:S(2)}) async-start(bf16[8,32,4096]{2,1,0:T(8,128)(2,1)} %bitcast.47), calls=%async_computation.2 | async-start | bytes 4194304 | tf_op jit(solution)/shard_map/all_to_all | solution.py:188
  76.4 5.1 %collective-permute-done.13 = bf16[384,256]{1,0:T(8,128)(2,1)S(1)} collective-permute-done((bf16[384,256]{1,0:T(8,128)(2,1)S(1)}, bf16[384,256]{1,0:T(8,128)(2,1)S(1)}, u32[]{:S(2)}, u32[]{:S(2)}) %collective-permute-start.13) | collective-permute-done | bytes 196640 | tf_op jit(solution)/shard_map/ppermute | solution.py:175
  81.6 3.2 %collective-permute-start.14 = (bf16[384,256]{1,0:T(8,128)(2,1)S(1)}, bf16[384,256]{1,0:T(8,128)(2,1)S(1)}, u32[]{:S(2)}, u32[]{:S(2)}) collective-permute-start(bf16[384,256]{1,0:T(8,128)(2,1)S(1)} %fusion), channel_id=1, source_target_pairs={{0,14},{2,0},{4,2},{6,4},{8,6},{10,8},{12,10},{14,12},{1,15},{3,1}... | collective-permute-start | bytes 589832 | tf_op jit(solution)/shard_map/ppermute | solution.py:175
  84.9 3.9 %collective-permute-done.14 = bf16[384,256]{1,0:T(8,128)(2,1)S(1)} collective-permute-done((bf16[384,256]{1,0:T(8,128)(2,1)S(1)}, bf16[384,256]{1,0:T(8,128)(2,1)S(1)}, u32[]{:S(2)}, u32[]{:S(2)}) %collective-permute-start.14) | collective-permute-done | bytes 196640 | tf_op jit(solution)/shard_map/ppermute | solution.py:175
  88.9 7.3 %collective-permute-start.18 = (bf16[128,256]{1,0:T(8,128)(2,1)S(1)}, bf16[128,256]{1,0:T(8,128)(2,1)S(1)}, u32[]{:S(2)}, u32[]{:S(2)}) collective-permute-start(bf16[128,256]{1,0:T(8,128)(2,1)S(1)} %slice.55), channel_id=1, source_target_pairs={{64,14},{66,0},{68,2},{70,4},{72,6},{74,8},{76,10},{78,12},{128,78... | collective-permute-start | bytes 196616 | tf_op jit(solution)/shard_map/ppermute | solution.py:184
  102.4 2.3 %collective-permute-done.17 = bf16[128,256]{1,0:T(8,128)(2,1)S(1)} collective-permute-done((bf16[128,256]{1,0:T(8,128)(2,1)S(1)}, bf16[128,256]{1,0:T(8,128)(2,1)S(1)}, u32[]{:S(2)}, u32[]{:S(2)}) %collective-permute-start.17) | collective-permute-done | bytes 65568 | tf_op jit(solution)/shard_map/ppermute | solution.py:184
  105.2 2.6 %collective-permute-done.12 = bf16[256,256]{1,0:T(8,128)(2,1)S(1)} collective-permute-done((bf16[256,256]{1,0:T(8,128)(2,1)S(1)}, bf16[256,256]{1,0:T(8,128)(2,1)S(1)}, u32[]{:S(2)}, u32[]{:S(2)}) %collective-permute-start.12) | collective-permute-done | bytes 131104 | tf_op jit(solution)/shard_map/ppermute | solution.py:175
  108.6 4.1 %all-to-all-start.3 = ((bf16[8,32,256]{2,1,0:T(8,128)(2,1)}), bf16[8,32,256]{2,1,0:T(8,128)(2,1)S(1)}, u32[]{:S(2)}, u32[]{:S(2)}) async-start(bf16[8,32,256]{2,1,0:T(8,128)(2,1)} %bitcast.23), calls=%async_computation.3 | async-start | bytes 262144 | tf_op jit(solution)/shard_map/all_to_all | solution.py:188
  112.6 2.6 %shard_map.87 = (bf16[32,16384]{1,0:T(8,128)(2,1)}, bf16[32,16384]{1,0:T(8,128)(2,1)}) custom-call(bf16[8,32,4096]{2,1,0:T(8,128)(2,1)} %copy-done), custom_call_target="tpu_custom_call" | custom-call | tf_op jit(solution)/shard_map/pallas_call | solution.py:223
  115.2 3.5 %all-to-all-done.3 = bf16[8,32,256]{2,1,0:T(8,128)(2,1)S(1)} async-done(((bf16[8,32,256]{2,1,0:T(8,128)(2,1)}), bf16[8,32,256]{2,1,0:T(8,128)(2,1)S(1)}, u32[]{:S(2)}, u32[]{:S(2)}) %all-to-all-start.3) | async-done | bytes 131104 | tf_op jit(solution)/shard_map/all_to_all | solution.py:188
  (82 shorter events, 20.3 us)
Async XLA Ops:
  2.2 10.4 %all-to-all-start = ((bf16[8,32,256]{2,1,0:T(8,128)(2,1)}), bf16[8,32,256]{2,1,0:T(8,128)(2,1)S(1)}, u32[]{:S(2)}, u32[]{:S(2)}) async-start(bf16[8,32,256]{2,1,0:T(8,128)(2,1)} %shard_map.84), calls=%async_computation | async-start | bytes 262144 | tf_op jit(solution)/shard_map/all_to_all | solution.py:188
  12.6 37.3 %all-to-all-start.1 = ((bf16[8,32,4096]{2,1,0:T(8,128)(2,1)}), bf16[8,32,4096]{2,1,0:T(8,128)(2,1)S(1)}, u32[]{:S(2)}, u32[]{:S(2)}) async-start(bf16[8,32,4096]{2,1,0:T(8,128)(2,1)} %shard_map.85), calls=%async_computation.1 | async-start | bytes 4194304 | tf_op jit(solution)/shard_map/all_to_all | solution.py:188
  16.2 6.3 %collective-permute-start = (bf16[128,256]{1,0:T(8,128)(2,1)S(1)}, bf16[128,256]{1,0:T(8,128)(2,1)S(1)}, u32[]{:S(2)}, u32[]{:S(2)}) collective-permute-start(bf16[128,256]{1,0:T(8,128)(2,1)S(1)} %bitcast.60), channel_id=1, source_target_pairs={{0,64},{64,128},{128,192},{1,65},{65,129},{129,193},{2,66},{66,130... | collective-permute-start | bytes 196616 | tf_op jit(solution)/shard_map/ppermute | solution.py:242
  22.6 33.4 %copy-start.2 = (bf16[384,256]{1,0:T(8,128)(2,1)}, bf16[384,256]{1,0:T(8,128)(2,1)S(1)}, u32[]{:S(2)}) copy-start(bf16[384,256]{1,0:T(8,128)(2,1)S(1)} %pad_maximum_fusion) | copy-start | bytes 589828
  22.6 9.9 %collective-permute-start.4 = (bf16[384,256]{1,0:T(8,128)(2,1)S(1)}, bf16[384,256]{1,0:T(8,128)(2,1)S(1)}, u32[]{:S(2)}, u32[]{:S(2)}) collective-permute-start(bf16[384,256]{1,0:T(8,128)(2,1)S(1)} %pad_maximum_fusion), channel_id=1, source_target_pairs={{0,14},{2,0},{4,2},{6,4},{8,6},{10,8},{12,10},{14,12},{1,15},{3,1}... | collective-permute-start | bytes 589832 | tf_op jit(solution)/shard_map/ppermute | solution.py:175
  28.5 7.7 %collective-permute-start.1 = (bf16[384,256]{1,0:T(8,128)(2,1)S(1)}, bf16[384,256]{1,0:T(8,128)(2,1)S(1)}, u32[]{:S(2)}, u32[]{:S(2)}) collective-permute-start(bf16[384,256]{1,0:T(8,128)(2,1)S(1)} %pad_maximum_fusion), channel_id=1, source_target_pairs={{0,2},{2,4},{4,6},{6,8},{8,10},{10,12},{12,14},{14,0},{1,3},{3,5},... | collective-permute-start | bytes 589832 | tf_op jit(solution)/shard_map/ppermute | solution.py:175
  32.5 6.9 %collective-permute-start.5 = (bf16[384,256]{1,0:T(8,128)(2,1)S(1)}, bf16[384,256]{1,0:T(8,128)(2,1)S(1)}, u32[]{:S(2)}, u32[]{:S(2)}) collective-permute-start(bf16[384,256]{1,0:T(8,128)(2,1)S(1)} %collective-permute-done.4), channel_id=1, source_target_pairs={{0,14},{2,0},{4,2},{6,4},{8,6},{10,8},{12,10},{14,12},{1,15},{3,1}... | collective-permute-start | bytes 589832 | tf_op jit(solution)/shard_map/ppermute | solution.py:175
  36.2 6.9 %collective-permute-start.2 = (bf16[384,256]{1,0:T(8,128)(2,1)S(1)}, bf16[384,256]{1,0:T(8,128)(2,1)S(1)}, u32[]{:S(2)}, u32[]{:S(2)}) collective-permute-start(bf16[384,256]{1,0:T(8,128)(2,1)S(1)} %collective-permute-done.1), channel_id=1, source_target_pairs={{0,2},{2,4},{4,6},{6,8},{8,10},{10,12},{12,14},{14,0},{1,3},{3,5},... | collective-permute-start | bytes 589832 | tf_op jit(solution)/shard_map/ppermute | solution.py:175
  39.4 6.9 %collective-permute-start.6 = (bf16[384,256]{1,0:T(8,128)(2,1)S(1)}, bf16[384,256]{1,0:T(8,128)(2,1)S(1)}, u32[]{:S(2)}, u32[]{:S(2)}) collective-permute-start(bf16[384,256]{1,0:T(8,128)(2,1)S(1)} %collective-permute-done.5), channel_id=1, source_target_pairs={{0,14},{2,0},{4,2},{6,4},{8,6},{10,8},{12,10},{14,12},{1,15},{3,1}... | collective-permute-start | bytes 589832 | tf_op jit(solution)/shard_map/ppermute | solution.py:175
  43.1 6.9 %collective-permute-start.3 = (bf16[384,256]{1,0:T(8,128)(2,1)S(1)}, bf16[384,256]{1,0:T(8,128)(2,1)S(1)}, u32[]{:S(2)}, u32[]{:S(2)}) collective-permute-start(bf16[384,256]{1,0:T(8,128)(2,1)S(1)} %collective-permute-done.2), channel_id=1, source_target_pairs={{0,2},{2,4},{4,6},{6,8},{8,10},{10,12},{12,14},{14,0},{1,3},{3,5},... | collective-permute-start | bytes 589832 | tf_op jit(solution)/shard_map/ppermute | solution.py:175
  50.0 4.7 %collective-permute-start.8 = (bf16[384,128]{1,0:T(8,128)(2,1)S(1)}, bf16[384,128]{1,0:T(8,128)(2,1)S(1)}, u32[]{:S(2)}, u32[]{:S(2)}) collective-permute-start(bf16[384,128]{1,0:T(8,128)(2,1)S(1)} %slice.43), channel_id=1, source_target_pairs={{0,14},{2,0},{4,2},{6,4},{8,6},{10,8},{12,10},{14,12},{1,15},{3,1}... | collective-permute-start | bytes 294920 | tf_op jit(solution)/shard_map/ppermute | solution.py:175
  50.1 5.9 %collective-permute-start.7 = (bf16[384,128]{1,0:T(8,128)(2,1)S(1)}, bf16[384,128]{1,0:T(8,128)(2,1)S(1)}, u32[]{:S(2)}, u32[]{:S(2)}) collective-permute-start(bf16[384,128]{1,0:T(8,128)(2,1)S(1)} %slice.42), channel_id=1, source_target_pairs={{0,2},{2,4},{4,6},{6,8},{8,10},{10,12},{12,14},{14,0},{1,3},{3,5},... | collective-permute-start | bytes 294920 | tf_op jit(solution)/shard_map/ppermute | solution.py:175
  68.3 7.8 %collective-permute-start.9 = (bf16[384,256]{1,0:T(8,128)(2,1)}, bf16[384,256]{1,0:T(8,128)(2,1)S(1)}, u32[]{:S(2)}, u32[]{:S(2)}) collective-permute-start(bf16[384,256]{1,0:T(8,128)(2,1)} %bitcast.62), channel_id=1, source_target_pairs={{0,2},{2,4},{4,6},{6,8},{8,10},{10,12},{12,14},{14,0},{1,3},{3,5},... | collective-permute-start | bytes 589832 | tf_op jit(solution)/shard_map/ppermute | solution.py:175
  69.7 38.8 %all-to-all-start.2 = ((bf16[8,32,4096]{2,1,0:T(8,128)(2,1)}), bf16[8,32,4096]{2,1,0:T(8,128)(2,1)S(1)}, u32[]{:S(2)}, u32[]{:S(2)}) async-start(bf16[8,32,4096]{2,1,0:T(8,128)(2,1)} %bitcast.47), calls=%async_computation.2 | async-start | bytes 4194304 | tf_op jit(solution)/shard_map/all_to_all | solution.py:188
  74.1 7.4 %collective-permute-start.13 = (bf16[384,256]{1,0:T(8,128)(2,1)S(1)}, bf16[384,256]{1,0:T(8,128)(2,1)S(1)}, u32[]{:S(2)}, u32[]{:S(2)}) collective-permute-start(bf16[384,256]{1,0:T(8,128)(2,1)S(1)} %bitcast.61), channel_id=1, source_target_pairs={{0,14},{2,0},{4,2},{6,4},{8,6},{10,8},{12,10},{14,12},{1,15},{3,1}... | collective-permute-start | bytes 589832 | tf_op jit(solution)/shard_map/ppermute | solution.py:175
  76.2 8.6 %collective-permute-start.10 = (bf16[384,256]{1,0:T(8,128)(2,1)S(1)}, bf16[384,256]{1,0:T(8,128)(2,1)S(1)}, u32[]{:S(2)}, u32[]{:S(2)}) collective-permute-start(bf16[384,256]{1,0:T(8,128)(2,1)S(1)} %fusion.2), channel_id=1, source_target_pairs={{0,2},{2,4},{4,6},{6,8},{8,10},{10,12},{12,14},{14,0},{1,3},{3,5},... | collective-permute-start | bytes 589832 | tf_op jit(solution)/shard_map/ppermute | solution.py:175
  81.6 7.2 %collective-permute-start.14 = (bf16[384,256]{1,0:T(8,128)(2,1)S(1)}, bf16[384,256]{1,0:T(8,128)(2,1)S(1)}, u32[]{:S(2)}, u32[]{:S(2)}) collective-permute-start(bf16[384,256]{1,0:T(8,128)(2,1)S(1)} %fusion), channel_id=1, source_target_pairs={{0,14},{2,0},{4,2},{6,4},{8,6},{10,8},{12,10},{14,12},{1,15},{3,1}... | collective-permute-start | bytes 589832 | tf_op jit(solution)/shard_map/ppermute | solution.py:175
  84.8 11.4 %collective-permute-start.11 = (bf16[384,256]{1,0:T(8,128)(2,1)S(1)}, bf16[384,256]{1,0:T(8,128)(2,1)S(1)}, u32[]{:S(2)}, u32[]{:S(2)}) collective-permute-start(bf16[384,256]{1,0:T(8,128)(2,1)S(1)} %fusion.3), channel_id=1, source_target_pairs={{0,2},{2,4},{4,6},{6,8},{8,10},{10,12},{12,14},{14,0},{1,3},{3,5},... | collective-permute-start | bytes 589832 | tf_op jit(solution)/shard_map/ppermute | solution.py:175
  88.9 13.5 %collective-permute-start.18 = (bf16[128,256]{1,0:T(8,128)(2,1)S(1)}, bf16[128,256]{1,0:T(8,128)(2,1)S(1)}, u32[]{:S(2)}, u32[]{:S(2)}) collective-permute-start(bf16[128,256]{1,0:T(8,128)(2,1)S(1)} %slice.55), channel_id=1, source_target_pairs={{64,14},{66,0},{68,2},{70,4},{72,6},{74,8},{76,10},{78,12},{128,78... | collective-permute-start | bytes 196616 | tf_op jit(solution)/shard_map/ppermute | solution.py:184
  96.3 8.4 %collective-permute-start.17 = (bf16[128,256]{1,0:T(8,128)(2,1)S(1)}, bf16[128,256]{1,0:T(8,128)(2,1)S(1)}, u32[]{:S(2)}, u32[]{:S(2)}) collective-permute-start(bf16[128,256]{1,0:T(8,128)(2,1)S(1)} %slice.49), channel_id=1, source_target_pairs={{64,2},{66,4},{68,6},{70,8},{72,10},{74,12},{76,14},{78,0},{128,66... | collective-permute-start | bytes 196616 | tf_op jit(solution)/shard_map/ppermute | solution.py:184
  98.2 6.9 %collective-permute-start.16 = (bf16[128,256]{1,0:T(8,128)(2,1)S(1)}, bf16[128,256]{1,0:T(8,128)(2,1)S(1)}, u32[]{:S(2)}, u32[]{:S(2)}) collective-permute-start(bf16[128,256]{1,0:T(8,128)(2,1)S(1)} %bitcast.59), channel_id=1, source_target_pairs={{64,0},{128,64},{192,128},{65,1},{129,65},{193,129},{66,2},{130,66... | collective-permute-start | bytes 196616 | tf_op jit(solution)/shard_map/ppermute | solution.py:267
  100.2 5.0 %collective-permute-start.15 = (bf16[256,256]{1,0:T(8,128)(2,1)S(1)}, bf16[256,256]{1,0:T(8,128)(2,1)S(1)}, u32[]{:S(2)}, u32[]{:S(2)}) collective-permute-start(bf16[256,256]{1,0:T(8,128)(2,1)S(1)} %slice.54), channel_id=1, source_target_pairs={{0,14},{2,0},{4,2},{6,4},{8,6},{10,8},{12,10},{14,12},{1,15},{3,1}... | collective-permute-start | bytes 393224 | tf_op jit(solution)/shard_map/ppermute | solution.py:175
  101.6 6.3 %collective-permute-start.12 = (bf16[256,256]{1,0:T(8,128)(2,1)S(1)}, bf16[256,256]{1,0:T(8,128)(2,1)S(1)}, u32[]{:S(2)}, u32[]{:S(2)}) collective-permute-start(bf16[256,256]{1,0:T(8,128)(2,1)S(1)} %slice.47), channel_id=1, source_target_pairs={{0,2},{2,4},{4,6},{6,8},{8,10},{10,12},{12,14},{14,0},{1,3},{3,5},... | collective-permute-start | bytes 393224 | tf_op jit(solution)/shard_map/ppermute | solution.py:175
  108.6 10.2 %all-to-all-start.3 = ((bf16[8,32,256]{2,1,0:T(8,128)(2,1)}), bf16[8,32,256]{2,1,0:T(8,128)(2,1)S(1)}, u32[]{:S(2)}, u32[]{:S(2)}) async-start(bf16[8,32,256]{2,1,0:T(8,128)(2,1)} %bitcast.23), calls=%async_computation.3 | async-start | bytes 262144 | tf_op jit(solution)/shard_map/all_to_all | solution.py:188
  (17 other events, 184.1 us)
